TPU v7x, 512 devices: a whole 4x4x16 slice. The times are simulated.
512 devices in a mesh: dom: 64 (over z_hi, y, x, core), sp: 8 (over z_lo).
Axes of the slice: x: 4, y: 4, z: 16 (z_hi: 2, z_lo: 8; z = z_hi * 8 + z_lo), core: 2. Of those that a mesh axis runs over, the one named last changes fastest.
Arguments:
- positions: float32 [3, 32768], P(None, ('dom', 'sp')), may hold values from -1 to 1
- neighbours: int32 [24, 32768], P(None, ('dom', 'sp')), may hold values from 0 to 1279, as said below
- counts: int32 [32768], P(('dom', 'sp')), may hold values from 12 to 24, as said below
- send_lists: int32 [64, 6, 128], P('dom'), may hold values from 0 to 511
- sparse_points: bfloat16 [16384, 512], P('sp'), may hold values from -0.25 to 0.25
- weights: float32 [16384], P('sp'), may hold values from -1280 to 1280
Outputs:
- energies: float32 [32768], P(('dom', 'sp'))
- forces: float32 [3, 32768], P(None, ('dom', 'sp'))
Inputs may be any that keep to these rules, and one draw needn't show every extreme that they name: `neighbours`: each atom's neighbour slots index its domain's table and never its own slot; slots at and beyond the atom's count are padding. `counts`: every device holds an atom with 24 live neighbours. `send_lists`: local indices of the sending domain's atoms; an atom may be sent through several faces.
All inputs are finite; a program needn't handle non-finite values.
Results may differ from a plain program's by a relative error of at most 0.0088.
Values may be sent and summed in bfloat16 or wider, within the bound.
A program may use at most 64 MiB of HBM per device.

v0:
```python
import math

import jax
import jax.numpy as jnp
import numpy as np
from jax import lax
from jax.experimental import pallas as pl
from jax.experimental.pallas import tpu as pltpu
from jax.sharding import PartitionSpec as P

F32, BF16 = jnp.float32, jnp.bfloat16
MESH = pl.DeviceIdType.MESH
SLOTS = 12
ROWS = 160
BACK = 176
CHUNK = 512


def powers():
    found, starts = [], []
    for degree in range(8):
        starts.append(len(found))
        for a in range(degree, -1, -1):
            for b in range(degree - a, -1, -1):
                found.append((a, b, degree - a - b))
    return found, starts + [len(found)]


POWERS, STARTS = powers()
PLACE = {p: i for i, p in enumerate(POWERS)}
SPREAD = [
    float(math.factorial(sum(p)) * math.prod(math.factorial(e) for e in p)) for p in POWERS
]


def raised(m, axis):
    p = list(POWERS[m])
    p[axis] += 1
    return PLACE[tuple(p)]


def expansion():
    e = np.zeros((2 * ROWS, 512), np.float32)
    for n in range(8):
        for n2 in range(8):
            for l in range(8):
                r = (n2 - n) % 8
                first = n
                if r > 4:
                    r, first = 8 - r, n2
                if r == 0:
                    group, half = 16 + l % 4, l // 4
                else:
                    group, half = {1: (l, 0), 3: (l, 1), 2: (8 + l, 0), 4: (8 + l, 1)}[r]
                e[half * ROWS + group * 8 + first, (n * 8 + n2) * 8 + l] = 1.0
    return e


def up(x, k):
    return x if k % 8 == 0 else pltpu.roll(x, (8 - k) % 8, 0)


def swap(x):
    return pltpu.roll(x, 64, 1)


def pieces(x, count):
    out = []
    for _ in range(count):
        p = x.astype(BF16).astype(F32)
        out.append(p)
        x = x - p
    return out


def one_hot(row):
    return jnp.where(lax.broadcasted_iota(jnp.int32, (128, 128), 0) == row, 1.0, 0.0).astype(BF16)


def kernel(
    faces, pos_ref, near_ref, count_ref, lists_ref, sparse_hbm, weight_ref, fold_hbm, spread_hbm,
    energy_ref, force_ref,
    posbuf, ghost_out, tab, pack, index, ohs, ohn, looked, offs, base, mono, radial, slope_r, dens,
    spec, dbuf, rbuf, gbuf, vbuf, descs, slopes, sparse, fold, spread, folded, wide, left, pulls,
    gtab, gret, domg, fin,
    local_sem, pos_s, pos_r, gho_s, gho_r, des_s, des_r, gra_s, gra_r, ret_s, ret_r, fin_s, fin_r,
):
    dom, sp = lax.axis_index("dom"), lax.axis_index("sp")
    n_dom, n_sp = lax.axis_size("dom"), lax.axis_size("sp")
    below = n_dom // 2
    ring = 2 * n_sp
    z = (dom // below) * n_sp + sp
    rest = lax.rem(dom, below)
    side = 1 - 2 * lax.rem(dom, 2)

    def along(delta):
        there = lax.rem(z + delta + ring, ring)
        return (rest + (there // n_sp) * below, lax.rem(there, n_sp))

    def peer(delta):
        return (dom, lax.rem(sp + delta, n_sp))

    def partner(face):
        bit = lax.rem(dom // 2**face, 2)
        return (dom + (1 - 2 * bit) * 2**face, sp)

    delta = [0, 1, -1, 2, -2, 3, -3, 4 * side]
    lane = lax.broadcasted_iota(jnp.int32, (8, 128), 1)
    low = lane < 64
    row8 = lax.broadcasted_iota(jnp.int32, (8, 128), 0)

    loads = [
        pltpu.make_async_copy(sparse_hbm, sparse, local_sem.at[0]),
        pltpu.make_async_copy(fold_hbm, fold, local_sem.at[1]),
        pltpu.make_async_copy(spread_hbm, spread, local_sem.at[2]),
    ]
    for load in loads:
        load.start()

    barrier = pltpu.get_barrier_semaphore()
    greeted = [peer(d) for d in range(1, 8)] + [partner(f) for f in range(faces)]
    greeted += [along(d) for d in (1, -1, 2, -2, 3, -3, 4, -4)]
    for who in greeted:
        pl.semaphore_signal(barrier, inc=1, device_id=who, device_id_type=MESH)

    posbuf[sp] = jnp.zeros((8, 128), F32)
    posbuf[sp, 0:3, 0:64] = pos_ref[...]
    here = posbuf[sp]
    here = here + swap(here)
    posbuf[sp] = here
    pl.semaphore_wait(barrier, len(greeted))

    def remote(src, dst, s, r, who):
        return pltpu.make_async_remote_copy(
            src_ref=src, dst_ref=dst, send_sem=s, recv_sem=r, device_id=who, device_id_type=MESH
        )

    sent_pos = [
        remote(posbuf.at[sp], posbuf.at[sp], pos_s.at[d - 1], pos_r.at[d - 1], peer(d))
        for d in range(1, 8)
    ]
    for c in sent_pos:
        c.start()

    for f in range(faces):
        ohs[:, f * 128 : (f + 1) * 128] = one_hot(lists_ref[f : f + 1, :] & 127)
    pack[...] = jnp.zeros((24, 128), jnp.int32)
    pack[:, 0:64] = near_ref[...]
    index[0:8] = jnp.where(low, pack[0:8], swap(pack[8:16]))
    last = pack[16:24]
    last = jnp.where(low, last, swap(pltpu.roll(last, 4, 0)))
    index[8:16] = jnp.where(row8 < 4, last, 0)
    for j in range(SLOTS):
        ohn[:, j * 128 : (j + 1) * 128] = one_hot(index[j : j + 1, :] & 127)

    for c in sent_pos:
        c.wait()

    for hi in range(4):
        tab[hi] = jnp.where(low, posbuf[2 * hi], posbuf[2 * hi + 1])

    own = tab[0:4].reshape(32, 128)
    parts = jnp.concatenate(pieces(own, 3), axis=0).astype(BF16)
    out = jnp.dot(parts, ohs[...], preferred_element_type=F32)
    out = out[0:32] + out[32:64] + out[64:96]
    sent_ghost = []
    for f in range(faces):
        which = lists_ref[f : f + 1, :] // 128
        tile = jnp.zeros((8, 128), F32)
        for hi in range(4):
            part = out[hi * 8 : hi * 8 + 8, f * 128 : (f + 1) * 128]
            tile = jnp.where(which == hi, part, tile)
        ghost_out[f] = tile
        c = remote(ghost_out.at[f], tab.at[4 + f], gho_s.at[f], gho_r.at[f], partner(f))
        c.start()
        sent_ghost.append(c)

    def look(first, last, into):
        n = (last - first) * 8
        values = tab[first:last].reshape(n, 128)
        split = jnp.concatenate(pieces(values, 3), axis=0).astype(BF16)
        for q in range(4):
            at = slice(q * 384, (q + 1) * 384)
            got = jnp.dot(split, ohn[:, at], preferred_element_type=F32)
            got = got[0:n] + got[n : 2 * n] + got[2 * n : 3 * n]
            for u in range(3):
                j = q * 3 + u
                which = index[j : j + 1, :] // 128
                tile = looked[j] if into else jnp.zeros((8, 128), F32)
                for hi in range(first, last):
                    part = got[(hi - first) * 8 : (hi - first) * 8 + 8, u * 128 : (u + 1) * 128]
                    tile = jnp.where(which == hi, part, tile)
                looked[j] = tile

    look(0, 4, False)
    for load in loads:
        load.wait()
    points = sparse.shape[0]

    @pl.loop(0, points // CHUNK)
    def _(c):
        at = pl.ds(pl.multiple_of(c * CHUNK, CHUNK), CHUNK)
        folded[:, at] = lax.dot_general(
            fold[...], sparse[at, :], (((1,), (1,)), ((), ())), preferred_element_type=F32
        ).astype(BF16)

    @pl.loop(0, points // 128)
    def _(c):
        column = jnp.broadcast_to(4.0 * weight_ref[pl.ds(c, 1), :], (128, 128)).T
        wide[pl.ds(pl.multiple_of(c * 128, 128), 128), :] = column

    for c in sent_ghost:
        c.wait()
    look(4, 4 + faces, True)

    offs[...] = jnp.zeros(offs.shape, F32)
    for j in range(SLOTS):
        offs[j] = 0.5 * (looked[j] - here)
    x, y, zz = offs[:, 0, :], offs[:, 1, :], offs[:, 2, :]
    squared = x * x + y * y + zz * zz
    j16 = lax.broadcasted_iota(jnp.int32, (16, 128), 0)
    h16 = lax.broadcasted_iota(jnp.int32, (16, 128), 1) // 64
    slot = jnp.where(j16 < 8, j16 + 8 * h16, 8 + j16 + 4 * h16)
    pack[0:8] = jnp.zeros((8, 128), jnp.int32)
    pack[0:1, 0:64] = count_ref[...]
    counts = pack[0:8]
    counts = (counts + swap(counts))[0:1]
    live = jnp.where((slot < counts) & (j16 < SLOTS), 1.0, 0.0)
    inside = 1.0 - squared * (1.0 / 3.5)
    base[0] = squared
    base[1] = inside * inside * live
    base[2] = (-2.0 / 3.5) * inside * live
    mono[0] = jnp.ones((16, 128), F32)
    for m in range(1, len(POWERS)):
        p = list(POWERS[m])
        axis = 2 if p[2] else 1 if p[1] else 0
        by = (x, y, zz)[axis] * (1.0 / p[axis])
        p[axis] -= 1
        mono[m] = mono[PLACE[tuple(p)]] * by
    centre = 0.05 + 0.15 * row8.astype(F32)
    for j in range(SLOTS):
        gap = base[0, j : j + 1, :] - centre
        bell = jnp.exp(-30.0 * gap * gap)
        r = bell * base[1, j : j + 1, :]
        radial[j] = r
        slope_r[j] = r * (-60.0 * gap) + bell * base[2, j : j + 1, :]

    @pl.loop(0, len(POWERS) // 8)
    def _(block):
        rs = [radial[j] for j in range(SLOTS)]
        for u in range(8):
            m = block * 8 + u
            rows = mono[m]
            total = rs[0] * rows[0:1, :]
            for j in range(1, SLOTS):
                total = total + rs[j] * rows[j : j + 1, :]
            dens[m] = total + swap(total)

    def turned(d):
        return jnp.where(low, d, up(d, 2))

    zero = []
    for l in range(8):
        s0 = s1 = s2 = None
        for m in range(STARTS[l], STARTS[l + 1]):
            d = dens[m]
            t = turned(d)
            f = d * SPREAD[m]
            a, b, c = f * d, f * up(t, 1), f * up(t, 2)
            s0, s1, s2 = (a, b, c) if s0 is None else (s0 + a, s1 + b, s2 + c)
        spec[l] = s1
        spec[8 + l] = s2
        zero.append(s0)
    for l in range(4):
        spec[16 + l] = jnp.where(low, zero[l], zero[l + 4])
    twice = jnp.where(low, 2.0, 1.0)

    def times(g):
        return 2.0 if g < 8 else twice if g < 16 else 1.0

    def both(tile):
        row = jnp.sum(tile, axis=0, keepdims=True)
        tile = jnp.broadcast_to(row, (8, 128))
        return tile + swap(tile)

    total = jnp.zeros((8, 128), F32)
    for g in range(20):
        v = spec[g]
        total = total + times(g) * v * v
    scale = lax.rsqrt(both(total) + 1e-06)
    for g in range(0, 20, 2):
        two = jnp.concatenate([spec[g] * scale, spec[g + 1] * scale], axis=0)
        dbuf[0, g * 8 : g * 8 + 16, :] = two.astype(BF16)

    sent_desc = [
        remote(dbuf.at[0], dbuf.at[t], des_s.at[t - 1], des_r.at[t - 1], along(delta[t]))
        for t in range(1, 8)
    ]
    for c in sent_desc:
        c.start()

    wlow = lax.broadcasted_iota(jnp.int32, (ROWS, 128), 1) < 64
    sent_grad = [None] * 8
    for slots in ((0, 1, 2, 3), (4, 5, 6, 7)):
        for t in slots:
            if t:
                sent_desc[t - 1].wait_recv()
        for k in range(2):
            xa = dbuf[slots[2 * k]].astype(F32)
            xb = dbuf[slots[2 * k + 1]].astype(F32)
            at = slice(k * 128, (k + 1) * 128)
            vbuf[0:ROWS, at] = jnp.where(wlow, xa, swap(xb)).astype(BF16)
            vbuf[ROWS : 2 * ROWS, at] = jnp.where(wlow, swap(xa), xb).astype(BF16)
        descs[...] = jnp.dot(spread[...], vbuf[...], preferred_element_type=F32).astype(BF16)
        energy = jnp.zeros((8, 256), F32)
        for c in range(points // CHUNK):
            at = slice(c * CHUNK, (c + 1) * CHUNK)
            score = jnp.dot(sparse[at, :], descs[...], preferred_element_type=F32)
            w = wide[at, :]
            square = score * score
            ws = jnp.concatenate([w, w], axis=1) * square
            energy = energy + jnp.sum((ws * square).reshape(CHUNK // 8, 8, 256), axis=0)
            slopes[at, :] = (ws * score).astype(BF16)
        energy = jnp.sum(energy, axis=0, keepdims=True)
        grad = jnp.dot(folded[...], slopes[...], preferred_element_type=F32)
        for k in range(2):
            a, b = slots[2 * k], slots[2 * k + 1]
            at = slice(k * 128, (k + 1) * 128)
            lo, hi = grad[0:ROWS, at], grad[ROWS : 2 * ROWS, at]
            rbuf[a, 0:ROWS, :] = jnp.where(wlow, lo, swap(hi)).astype(BF16)
            rbuf[b, 0:ROWS, :] = jnp.where(wlow, swap(lo), hi).astype(BF16)
            e = jnp.broadcast_to(energy[:, at], (8, 128))
            for t, mine in ((a, e), (b, swap(e))):
                p = pieces(mine, 3)
                tile = jnp.where(row8 == 0, p[0], jnp.where(row8 == 1, p[1], jnp.where(row8 == 2, p[2], 0.0)))
                tile = jnp.concatenate([tile, jnp.zeros((8, 128), F32)], axis=0)
                rbuf[t, ROWS:BACK, :] = tile.astype(BF16)
        for t in slots:
            if t:
                c = remote(rbuf.at[t], gbuf.at[t - 1], gra_s.at[t - 1], gra_r.at[t - 1], along(-delta[t]))
                c.start()
                sent_grad[t] = c

    summed = rbuf[0].astype(F32)
    for t in range(1, 8):
        sent_grad[t].wait_recv()
        summed = summed + gbuf[t - 1].astype(F32)
    last = summed[ROWS : ROWS + 8, :]
    energy_ref[...] = (0.25 * jnp.sum(last, axis=0, keepdims=True))[:, 0:64]

    dot = jnp.zeros((8, 128), F32)
    for g in range(20):
        dot = dot + summed[g * 8 : g * 8 + 8, :] * spec[g]
    dot = both(dot) * scale
    pull = []
    for g in range(20):
        pull.append(scale * (summed[g * 8 : g * 8 + 8, :] - times(g) * (spec[g] * scale) * dot))
    for l in range(8):
        ha, hb, h0 = pull[l], pull[8 + l], pull[16 + l % 4]
        h0 = swap(h0) if l < 4 else h0
        other = swap(ha)
        k1 = ha
        k2 = jnp.where(low, hb, hb + up(hb, 4))
        k5 = jnp.where(low, up(other, -3), up(other, -1))
        k6 = jnp.where(low, up(hb, -2), 2.0 * h0)
        for m in range(STARTS[l], STARTS[l + 1]):
            t = turned(dens[m])
            v = k1 * up(t, 1) + k2 * up(t, 2) + (k5 * up(t, 5) + k6 * up(t, 6))
            left[m] = (v + swap(v)) * SPREAD[m]

    @pl.loop(0, SLOTS // 4)
    def _(block):
        q = [[None] * 4 for _ in range(4)]

        def add(old, new):
            return new if old is None else old + new

        for m in range(len(POWERS)):
            d = [left[m]]
            if m < STARTS[7]:
                d += [left[raised(m, axis)] for axis in range(3)]
            for u in range(4):
                b = mono[m, pl.ds(block * 4 + u, 1), :]
                for axis in range(len(d)):
                    q[axis][u] = add(q[axis][u], d[axis] * b)
        for u in range(4):
            j = block * 4 + u
            r = radial[j]
            by_square = jnp.sum(slope_r[j] * q[0][u], axis=0, keepdims=True)
            gx, gy, gz = (jnp.sum(r * q[axis][u], axis=0, keepdims=True) for axis in (1, 2, 3))
            straight = jnp.where(row8 == 0, gx, jnp.where(row8 == 1, gy, jnp.where(row8 == 2, gz, 0.0)))
            pulls[j] = 0.5 * straight + offs[j] * by_square

    centre_grad = pulls[0]
    for j in range(1, SLOTS):
        centre_grad = centre_grad + pulls[j]
    centre_grad = centre_grad + swap(centre_grad)

    def placed(tiles, which, first, last):
        rows = []
        split = [pieces(tile, 2) for tile in tiles]
        for p in range(2):
            for hi in range(first, last):
                rows.append(jnp.concatenate(
                    [jnp.where(w == hi, s[p], 0.0) for w, s in zip(which, split)], axis=1
                ))
        return jnp.concatenate(rows, axis=0).astype(BF16)

    over_lanes = (((1,), (1,)), ((), ()))

    def scatter(first, last):
        n = (last - first) * 8
        total = jnp.zeros((n, 128), F32)
        for q in range(4):
            js = range(q * 3, q * 3 + 3)
            which = [index[j : j + 1, :] // 128 for j in js]
            rows = placed([pulls[j] for j in js], which, first, last)
            got = lax.dot_general(
                rows, ohn[:, q * 384 : (q + 1) * 384], over_lanes, preferred_element_type=F32
            )
            total = total + got[0:n] + got[n : 2 * n]
        return total.reshape(last - first, 8, 128)

    gtab[4 : 4 + faces] = scatter(4, 4 + faces)
    sent_back = []
    for f in range(faces):
        c = remote(gtab.at[4 + f], gret.at[f], ret_s.at[f], ret_r.at[f], partner(f))
        c.start()
        sent_back.append(c)
    own = scatter(0, 4)
    for c in sent_back:
        c.wait_recv()
    which = [lists_ref[f : f + 1, :] // 128 for f in range(faces)]
    rows = placed([gret[f] for f in range(faces)], which, 0, 4)
    got = lax.dot_general(rows, ohs[...], over_lanes, preferred_element_type=F32)
    domg[...] = own + (got[0:32] + got[32:64]).reshape(4, 8, 128)
    sent_fin = []
    for d in range(1, 8):
        who = peer(d)
        c = remote(domg.at[who[1] // 2], fin.at[d - 1], fin_s.at[d - 1], fin_r.at[d - 1], who)
        c.start()
        sent_fin.append(c)
    mine = domg[sp // 2]
    for d in range(1, 8):
        sent_fin[d - 1].wait_recv()
        mine = mine + fin[d - 1]
    odd = jnp.where(lax.rem(sp, 2) == 1, 1, 0)
    mine = jnp.where(odd == 1, swap(mine), mine)
    force_ref[...] = (centre_grad - mine)[0:3, 0:64]
    for c in sent_desc + sent_grad[1:] + sent_back + sent_fin:
        c.wait_send()


def body(positions, neighbours, counts, send_lists, sparse_points, weights):
    faces = send_lists.shape[1]
    points = sparse_points.shape[0]
    fold = expansion()
    vmem = pl.BlockSpec(memory_space=pltpu.VMEM)
    hbm = pl.BlockSpec(memory_space=pl.ANY)
    dma = pltpu.SemaphoreType.DMA
    energies, forces = pl.pallas_call(
        lambda *refs: kernel(faces, *refs),
        out_shape=(
            jax.ShapeDtypeStruct((1, 64), F32),
            jax.ShapeDtypeStruct((3, 64), F32),
        ),
        in_specs=[vmem, vmem, vmem, vmem, hbm, vmem, hbm, hbm],
        out_specs=(vmem, vmem),
        scratch_shapes=[
            pltpu.VMEM((8, 8, 128), F32),
            pltpu.VMEM((faces, 8, 128), F32),
            pltpu.VMEM((4 + faces, 8, 128), F32),
            pltpu.VMEM((24, 128), jnp.int32),
            pltpu.VMEM((16, 128), jnp.int32),
            pltpu.VMEM((128, faces * 128), BF16),
            pltpu.VMEM((128, SLOTS * 128), BF16),
            pltpu.VMEM((SLOTS, 8, 128), F32),
            pltpu.VMEM((16, 8, 128), F32),
            pltpu.VMEM((3, 16, 128), F32),
            pltpu.VMEM((120, 16, 128), F32),
            pltpu.VMEM((SLOTS, 8, 128), F32),
            pltpu.VMEM((SLOTS, 8, 128), F32),
            pltpu.VMEM((120, 8, 128), F32),
            pltpu.VMEM((20, 8, 128), F32),
            pltpu.VMEM((8, ROWS, 128), BF16),
            pltpu.VMEM((8, BACK, 128), BF16),
            pltpu.VMEM((7, BACK, 128), BF16),
            pltpu.VMEM((2 * ROWS, 256), BF16),
            pltpu.VMEM((512, 256), BF16),
            pltpu.VMEM((points, 256), BF16),
            pltpu.VMEM((points, 512), BF16),
            pltpu.VMEM((2 * ROWS, 512), BF16),
            pltpu.VMEM((512, 2 * ROWS), BF16),
            pltpu.VMEM((2 * ROWS, points), BF16),
            pltpu.VMEM((points, 128), F32),
            pltpu.VMEM((120, 8, 128), F32),
            pltpu.VMEM((SLOTS, 8, 128), F32),
            pltpu.VMEM((4 + faces, 8, 128), F32),
            pltpu.VMEM((faces, 8, 128), F32),
            pltpu.VMEM((4, 8, 128), F32),
            pltpu.VMEM((7, 8, 128), F32),
            dma((3,)),
            dma((7,)), dma((7,)),
            dma((faces,)), dma((faces,)),
            dma((7,)), dma((7,)),
            dma((7,)), dma((7,)),
            dma((faces,)), dma((faces,)),
            dma((7,)), dma((7,)),
        ],
        compiler_params=pltpu.CompilerParams(
            collective_id=0, has_side_effects=True, vmem_limit_bytes=48 * 2**20
        ),
        name="gap_forces",
    )(
        positions,
        neighbours,
        counts.reshape(1, -1),
        send_lists[0],
        sparse_points,
        weights.reshape(-1, 128),
        jnp.asarray(fold, BF16),
        jnp.asarray(fold.T, BF16),
    )
    return energies.reshape(-1), forces


def solution(mesh):
    in_specs = (
        P(None, ("dom", "sp")),
        P(None, ("dom", "sp")),
        P(("dom", "sp")),
        P("dom", None, None),
        P("sp", None),
        P("sp"),
    )
    out_specs = (P(("dom", "sp")), P(None, ("dom", "sp")))
    return jax.shard_map(body, mesh=mesh, in_specs=in_specs, out_specs=out_specs, check_vma=False)
```

profile of v0, /device:TPU:18, one launch (start us, length us, event | category | flops | bytes accessed | tf_op | source)
XLA Modules:
  0.0 73.5 jit_solution(16823262112782921424)
XLA Ops:
  0.6 0.7 copy.12
  1.3 0.0 copy-start
  1.3 1.6 %copy-done = bf16[2048,512]{1,0:T(8,128)(2,1)S(1)} copy-done((bf16[2048,512]{1,0:T(8,128)(2,1)S(1)}, bf16[2048,512]{1,0:T(8,128)(2,1)}, u32[]{:S(2)}) %copy-start) | copy-done | bytes 2097176
  2.9 0.0 copy-start.1
  2.9 1.0 %copy-done.1 = bf16[512,320]{1,0:T(8,128)(2,1)S(1)} copy-done((bf16[512,320]{1,0:T(8,128)(2,1)S(1)}, bf16[512,320]{1,0:T(8,128)(2,1)}, u32[]{:S(2)}) %copy-start.1) | copy-done | bytes 327704
  3.9 0.0 copy-start.2
  3.9 1.0 %copy-done.2 = bf16[320,512]{1,0:T(8,128)(2,1)S(1)} copy-done((bf16[320,512]{1,0:T(8,128)(2,1)S(1)}, bf16[320,512]{1,0:T(8,128)(2,1)}, u32[]{:S(2)}) %copy-start.2) | copy-done | bytes 327704
  4.9 0.0 copy-start.3
  4.9 0.7 copy-done.3
  5.6 0.0 copy-start.4
  5.6 0.7 copy-done.4
  6.3 0.0 copy-start.5
  6.3 0.7 copy-done.5
  7.0 0.0 copy-start.6
  7.0 0.7 copy-done.6
  7.6 64.7 %gap_forces.1 = (f32[1,64]{1,0:T(1,128)S(1)}, f32[3,64]{1,0:T(4,128)S(1)}) custom-call(f32[3,64]{1,0:T(4,128)S(1)} %copy-done.5, s32[24,64]{1,0:T(8,128)S(1)} %copy-done.3, s32[1,64]{1,0:T(1,128)S(1)} %bitcast.8, s32[6,128]{1,0:T(8,128)S(1)} %bitcast.6, bf16[2048,512]{1,0:T(8,128)(2,1)S(1)} %copy-done, f32[16,128]{1,0:T(8,128)S(1)} %bitcast.7, ...), custom_call_target="tpu_custom_call" | custom-call | tf_op jit(solution)/shard_map/gap_forces/pallas_call | solution.py:461
  72.4 0.5 copy.15
  72.9 0.6 copy.16
Async XLA Ops:
  1.3 1.6 %copy-start = (bf16[2048,512]{1,0:T(8,128)(2,1)S(1)}, bf16[2048,512]{1,0:T(8,128)(2,1)}, u32[]{:S(2)}) copy-start(bf16[2048,512]{1,0:T(8,128)(2,1)} %refs_4_.1) | copy-start | bytes 6291460
  2.9 1.0 %copy-start.1 = (bf16[512,320]{1,0:T(8,128)(2,1)S(1)}, bf16[512,320]{1,0:T(8,128)(2,1)}, u32[]{:S(2)}) copy-start(bf16[512,320]{1,0:T(8,128)(2,1)} %constant.5.clone.refs_7_) | copy-start | bytes 983044
  3.9 1.0 %copy-start.2 = (bf16[320,512]{1,0:T(8,128)(2,1)S(1)}, bf16[320,512]{1,0:T(8,128)(2,1)}, u32[]{:S(2)}) copy-start(bf16[320,512]{1,0:T(8,128)(2,1)} %constant.4.clone.refs_6_) | copy-start | bytes 983044
  4.9 0.7 copy-start.3
  5.6 0.7 copy-start.4
  6.3 0.7 copy-start.5
  7.0 0.7 copy-start.6
where the time goes:
time: 73.8 us; the launch traced here: 73.5 us
  Pallas kernels  64.7 us (88%)
  local copies, waits for them, and re-layouts  8.07 us (11%)
    pallas_call x1, Pallas kernels, body(): pl.pallas_call(lambda *refs: kernel(faces, *refs), out_shape=(jax.ShapeDt...  64.7 us
    unnamed x17, local copies, waits for them, and re-layouts  8.07 us

commit v1 on v0

--- a/solution.py
+++ b/solution.py
@@ -2,7 +2,6 @@
 
 import jax
 import jax.numpy as jnp
-import numpy as np
 from jax import lax
 from jax.experimental import pallas as pl
 from jax.experimental.pallas import tpu as pltpu
@@ -39,21 +38,14 @@
     return PLACE[tuple(p)]
 
 
-def expansion():
-    e = np.zeros((2 * ROWS, 512), np.float32)
-    for n in range(8):
-        for n2 in range(8):
-            for l in range(8):
-                r = (n2 - n) % 8
-                first = n
-                if r > 4:
-                    r, first = 8 - r, n2
-                if r == 0:
-                    group, half = 16 + l % 4, l // 4
-                else:
-                    group, half = {1: (l, 0), 3: (l, 1), 2: (8 + l, 0), 4: (8 + l, 1)}[r]
-                e[half * ROWS + group * 8 + first, (n * 8 + n2) * 8 + l] = 1.0
-    return e
+def packed_place(e):
+    n, n2, l = e // 64, (e // 8) & 7, e & 7
+    r = (n2 - n) & 7
+    first = jnp.where(r > 4, n2, n)
+    r = jnp.where(r > 4, 8 - r, r)
+    group = jnp.where(r == 0, 16 + (l & 3), jnp.where((r & 1) == 1, l, 8 + l))
+    half = jnp.where(r == 0, l // 4, jnp.where(r > 2, 1, 0))
+    return half * ROWS + group * 8 + first
 
 
 def up(x, k):
@@ -78,12 +70,13 @@
 
 
 def kernel(
-    faces, pos_ref, near_ref, count_ref, lists_ref, sparse_hbm, weight_ref, fold_hbm, spread_hbm,
+    faces, pos_hbm, near_hbm, count_hbm, lists_hbm, sparse_hbm, weight_hbm,
     energy_ref, force_ref,
-    posbuf, ghost_out, tab, pack, index, ohs, ohn, looked, offs, base, mono, radial, slope_r, dens,
+    pos_ref, near_ref, count_ref, lists_ref, weight_ref,
+    posbuf, topbuf, ghost_out, tab, pack, index, ohs, oht, ohn, looked, offs, base, mono, radial, slope_r, dens,
     spec, dbuf, rbuf, gbuf, vbuf, descs, slopes, sparse, fold, spread, folded, wide, left, pulls,
-    gtab, gret, domg, fin,
-    local_sem, pos_s, pos_r, gho_s, gho_r, des_s, des_r, gra_s, gra_r, ret_s, ret_r, fin_s, fin_r,
+    gtab, gret, domg, fin, topg, fintop,
+    local_sem, pos_s, pos_r, top_s, top_r, gho_s, gho_r, des_s, des_r, gra_s, gra_r, ret_s, ret_r, fin_s, fin_r, fit_s, fit_r,
 ):
     dom, sp = lax.axis_index("dom"), lax.axis_index("sp")
     n_dom, n_sp = lax.axis_size("dom"), lax.axis_size("sp")
@@ -109,41 +102,36 @@
     low = lane < 64
     row8 = lax.broadcasted_iota(jnp.int32, (8, 128), 0)
 
-    loads = [
-        pltpu.make_async_copy(sparse_hbm, sparse, local_sem.at[0]),
-        pltpu.make_async_copy(fold_hbm, fold, local_sem.at[1]),
-        pltpu.make_async_copy(spread_hbm, spread, local_sem.at[2]),
+    def above(d):
+        return (lax.rem(dom + below, n_dom), lax.rem(sp + d, n_sp))
+
+    pairs = [
+        (pos_hbm, pos_ref), (lists_hbm, lists_ref), (near_hbm, near_ref), (count_hbm, count_ref),
+        (weight_hbm, weight_ref), (sparse_hbm, sparse),
     ]
+    loads = [pltpu.make_async_copy(a, b, local_sem.at[i]) for i, (a, b) in enumerate(pairs)]
     for load in loads:
         load.start()
 
     barrier = pltpu.get_barrier_semaphore()
-    greeted = [peer(d) for d in range(1, 8)] + [partner(f) for f in range(faces)]
-    greeted += [along(d) for d in (1, -1, 2, -2, 3, -3, 4, -4)]
+    greeted = [peer(d) for d in range(1, 8)] + [partner(f) for f in range(faces - 1)]
+    greeted += [along(d) for d in (1, -1, 2, -2, 3, -3, 4, -4)] + [above(d) for d in range(8)]
     for who in greeted:
         pl.semaphore_signal(barrier, inc=1, device_id=who, device_id_type=MESH)
 
+    loads[0].wait()
+    loads[1].wait()
+    top = faces - 1
     posbuf[sp] = jnp.zeros((8, 128), F32)
     posbuf[sp, 0:3, 0:64] = pos_ref[...]
     here = posbuf[sp]
     here = here + swap(here)
+    here = jnp.where(row8 == 3, lists_ref[top].astype(F32), here)
     posbuf[sp] = here
-    pl.semaphore_wait(barrier, len(greeted))
-
-    def remote(src, dst, s, r, who):
-        return pltpu.make_async_remote_copy(
-            src_ref=src, dst_ref=dst, send_sem=s, recv_sem=r, device_id=who, device_id_type=MESH
-        )
-
-    sent_pos = [
-        remote(posbuf.at[sp], posbuf.at[sp], pos_s.at[d - 1], pos_r.at[d - 1], peer(d))
-        for d in range(1, 8)
-    ]
-    for c in sent_pos:
-        c.start()
-
-    for f in range(faces):
-        ohs[:, f * 128 : (f + 1) * 128] = one_hot(lists_ref[f : f + 1, :] & 127)
+    for load in loads[2:5]:
+        load.wait()
+    for f in range(top):
+        ohs[:, f * 128 : (f + 1) * 128] = one_hot(lists_ref[f] & 127)
     pack[...] = jnp.zeros((24, 128), jnp.int32)
     pack[:, 0:64] = near_ref[...]
     index[0:8] = jnp.where(low, pack[0:8], swap(pack[8:16]))
@@ -152,6 +140,49 @@
     index[8:16] = jnp.where(row8 < 4, last, 0)
     for j in range(SLOTS):
         ohn[:, j * 128 : (j + 1) * 128] = one_hot(index[j : j + 1, :] & 127)
+    pl.semaphore_wait(barrier, len(greeted))
+
+    def remote(src, dst, s, r, who):
+        return pltpu.make_async_remote_copy(
+            src_ref=src, dst_ref=dst, send_sem=s, recv_sem=r, device_id=who, device_id_type=MESH
+        )
+
+    sent_pos = [
+        remote(posbuf.at[sp], posbuf.at[sp], pos_s.at[d - 1], pos_r.at[d - 1], peer(d))
+        for d in range(1, 8)
+    ]
+    for c in sent_pos:
+        c.start()
+
+    sent_top = [
+        remote(posbuf.at[sp], topbuf.at[sp], top_s.at[d], top_r.at[d], above(d)) for d in range(8)
+    ]
+    for c in sent_top:
+        c.start()
+
+    place = packed_place(lax.broadcasted_iota(jnp.int32, (8, 512), 1))[0:1]
+    numbers = lax.broadcasted_iota(jnp.int32, (2 * ROWS, 512), 0)
+    fold[...] = jnp.where(numbers == place, 1.0, 0.0).astype(BF16)
+    place = packed_place(lax.broadcasted_iota(jnp.int32, (512, 128), 0))
+    for k in range(0, 2 * ROWS, 128):
+        n = min(128, 2 * ROWS - k)
+        numbers = k + lax.broadcasted_iota(jnp.int32, (512, 128), 1)
+        spread[:, k : k + n] = jnp.where(numbers == place, 1.0, 0.0).astype(BF16)[:, 0:n]
+    for load in loads[5:]:
+        load.wait()
+    points = sparse.shape[0]
+
+    @pl.loop(0, points // 128)
+    def _(c):
+        column = jnp.broadcast_to(4.0 * weight_ref[pl.ds(c, 1), :], (128, 128)).T
+        wide[pl.ds(pl.multiple_of(c * 128, 128), 128), :] = column
+
+    @pl.loop(0, points // CHUNK)
+    def _(c):
+        at = pl.ds(pl.multiple_of(c * CHUNK, CHUNK), CHUNK)
+        folded[:, at] = lax.dot_general(
+            fold[...], sparse[at, :], (((1,), (1,)), ((), ())), preferred_element_type=F32
+        ).astype(BF16)
 
     for c in sent_pos:
         c.wait()
@@ -159,18 +190,21 @@
     for hi in range(4):
         tab[hi] = jnp.where(low, posbuf[2 * hi], posbuf[2 * hi + 1])
 
-    own = tab[0:4].reshape(32, 128)
-    parts = jnp.concatenate(pieces(own, 3), axis=0).astype(BF16)
-    out = jnp.dot(parts, ohs[...], preferred_element_type=F32)
-    out = out[0:32] + out[32:64] + out[64:96]
-    sent_ghost = []
-    for f in range(faces):
-        which = lists_ref[f : f + 1, :] // 128
+    def gather(tiles, hots):
+        parts = jnp.concatenate(pieces(tiles.reshape(32, 128), 3), axis=0).astype(BF16)
+        out = jnp.dot(parts, hots, preferred_element_type=F32)
+        return out[0:32] + out[32:64] + out[64:96]
+
+    def chosen(out, which):
         tile = jnp.zeros((8, 128), F32)
         for hi in range(4):
-            part = out[hi * 8 : hi * 8 + 8, f * 128 : (f + 1) * 128]
-            tile = jnp.where(which == hi, part, tile)
-        ghost_out[f] = tile
+            tile = jnp.where(which == hi, out[hi * 8 : hi * 8 + 8], tile)
+        return tile
+
+    out = gather(tab[0:4], ohs[...])
+    sent_ghost = []
+    for f in range(top):
+        ghost_out[f] = chosen(out[:, f * 128 : (f + 1) * 128], lists_ref[f] // 128)
         c = remote(ghost_out.at[f], tab.at[4 + f], gho_s.at[f], gho_r.at[f], partner(f))
         c.start()
         sent_ghost.append(c)
@@ -193,21 +227,14 @@
                 looked[j] = tile
 
     look(0, 4, False)
-    for load in loads:
-        load.wait()
-    points = sparse.shape[0]
-
-    @pl.loop(0, points // CHUNK)
-    def _(c):
-        at = pl.ds(pl.multiple_of(c * CHUNK, CHUNK), CHUNK)
-        folded[:, at] = lax.dot_general(
-            fold[...], sparse[at, :], (((1,), (1,)), ((), ())), preferred_element_type=F32
-        ).astype(BF16)
-
-    @pl.loop(0, points // 128)
-    def _(c):
-        column = jnp.broadcast_to(4.0 * weight_ref[pl.ds(c, 1), :], (128, 128)).T
-        wide[pl.ds(pl.multiple_of(c * 128, 128), 128), :] = column
+    for c in sent_top:
+        c.wait()
+    far = jnp.concatenate(
+        [jnp.where(low, topbuf[2 * hi], topbuf[2 * hi + 1]) for hi in range(4)], axis=0
+    )
+    top_list = topbuf[sp, 3:4, :].astype(jnp.int32)
+    oht[...] = one_hot(top_list & 127)
+    tab[4 + top] = chosen(gather(far, oht[...]), top_list // 128)
 
     for c in sent_ghost:
         c.wait()
@@ -296,8 +323,8 @@
         remote(dbuf.at[0], dbuf.at[t], des_s.at[t - 1], des_r.at[t - 1], along(delta[t]))
         for t in range(1, 8)
     ]
-    for c in sent_desc:
-        c.start()
+    for t in (7, 5, 6, 3, 4, 1, 2):
+        sent_desc[t - 1].start()
 
     wlow = lax.broadcasted_iota(jnp.int32, (ROWS, 128), 1) < 64
     sent_grad = [None] * 8
@@ -423,17 +450,29 @@
 
     gtab[4 : 4 + faces] = scatter(4, 4 + faces)
     sent_back = []
-    for f in range(faces):
+    for f in range(top):
         c = remote(gtab.at[4 + f], gret.at[f], ret_s.at[f], ret_r.at[f], partner(f))
         c.start()
         sent_back.append(c)
+
+    def home(tiles, which, hots):
+        got = lax.dot_general(
+            placed(tiles, which, 0, 4), hots, over_lanes, preferred_element_type=F32
+        )
+        return (got[0:32] + got[32:64]).reshape(4, 8, 128)
+
+    topg[...] = home([gtab[4 + top]], [top_list // 128], oht[...])
+    sent_top = []
+    for d in range(8):
+        who = above(d)
+        c = remote(topg.at[who[1] // 2], fintop.at[d], fit_s.at[d], fit_r.at[d], who)
+        c.start()
+        sent_top.append(c)
     own = scatter(0, 4)
     for c in sent_back:
         c.wait_recv()
-    which = [lists_ref[f : f + 1, :] // 128 for f in range(faces)]
-    rows = placed([gret[f] for f in range(faces)], which, 0, 4)
-    got = lax.dot_general(rows, ohs[...], over_lanes, preferred_element_type=F32)
-    domg[...] = own + (got[0:32] + got[32:64]).reshape(4, 8, 128)
+    which = [lists_ref[f] // 128 for f in range(top)]
+    domg[...] = own + home([gret[f] for f in range(top)], which, ohs[...])
     sent_fin = []
     for d in range(1, 8):
         who = peer(d)
@@ -441,20 +480,22 @@
         c.start()
         sent_fin.append(c)
     mine = domg[sp // 2]
+    for d in range(8):
+        sent_top[d].wait_recv()
+        mine = mine + fintop[d]
     for d in range(1, 8):
         sent_fin[d - 1].wait_recv()
         mine = mine + fin[d - 1]
     odd = jnp.where(lax.rem(sp, 2) == 1, 1, 0)
     mine = jnp.where(odd == 1, swap(mine), mine)
     force_ref[...] = (centre_grad - mine)[0:3, 0:64]
-    for c in sent_desc + sent_grad[1:] + sent_back + sent_fin:
+    for c in sent_desc + sent_grad[1:] + sent_back + sent_top + sent_fin:
         c.wait_send()
 
 
 def body(positions, neighbours, counts, send_lists, sparse_points, weights):
     faces = send_lists.shape[1]
     points = sparse_points.shape[0]
-    fold = expansion()
     vmem = pl.BlockSpec(memory_space=pltpu.VMEM)
     hbm = pl.BlockSpec(memory_space=pl.ANY)
     dma = pltpu.SemaphoreType.DMA
@@ -464,15 +505,22 @@
             jax.ShapeDtypeStruct((1, 64), F32),
             jax.ShapeDtypeStruct((3, 64), F32),
         ),
-        in_specs=[vmem, vmem, vmem, vmem, hbm, vmem, hbm, hbm],
+        in_specs=[hbm] * 6,
         out_specs=(vmem, vmem),
         scratch_shapes=[
+            pltpu.VMEM(positions.shape, F32),
+            pltpu.VMEM(neighbours.shape, jnp.int32),
+            pltpu.VMEM((1, counts.shape[0]), jnp.int32),
+            pltpu.VMEM((faces, 1, 128), jnp.int32),
+            pltpu.VMEM((points // 128, 128), F32),
             pltpu.VMEM((8, 8, 128), F32),
-            pltpu.VMEM((faces, 8, 128), F32),
+            pltpu.VMEM((8, 8, 128), F32),
+            pltpu.VMEM((faces - 1, 8, 128), F32),
             pltpu.VMEM((4 + faces, 8, 128), F32),
             pltpu.VMEM((24, 128), jnp.int32),
             pltpu.VMEM((16, 128), jnp.int32),
-            pltpu.VMEM((128, faces * 128), BF16),
+            pltpu.VMEM((128, (faces - 1) * 128), BF16),
+            pltpu.VMEM((128, 128), BF16),
             pltpu.VMEM((128, SLOTS * 128), BF16),
             pltpu.VMEM((SLOTS, 8, 128), F32),
             pltpu.VMEM((16, 8, 128), F32),
@@ -496,30 +544,32 @@
             pltpu.VMEM((120, 8, 128), F32),
             pltpu.VMEM((SLOTS, 8, 128), F32),
             pltpu.VMEM((4 + faces, 8, 128), F32),
-            pltpu.VMEM((faces, 8, 128), F32),
+            pltpu.VMEM((faces - 1, 8, 128), F32),
             pltpu.VMEM((4, 8, 128), F32),
             pltpu.VMEM((7, 8, 128), F32),
-            dma((3,)),
+            pltpu.VMEM((4, 8, 128), F32),
+            pltpu.VMEM((8, 8, 128), F32),
+            dma((6,)),
             dma((7,)), dma((7,)),
-            dma((faces,)), dma((faces,)),
+            dma((8,)), dma((8,)),
+            dma((faces - 1,)), dma((faces - 1,)),
             dma((7,)), dma((7,)),
             dma((7,)), dma((7,)),
-            dma((faces,)), dma((faces,)),
+            dma((faces - 1,)), dma((faces - 1,)),
             dma((7,)), dma((7,)),
+            dma((8,)), dma((8,)),
         ],
         compiler_params=pltpu.CompilerParams(
-            collective_id=0, has_side_effects=True, vmem_limit_bytes=48 * 2**20
+            collective_id=0, has_side_effects=True, vmem_limit_bytes=60 * 2**20
         ),
         name="gap_forces",
     )(
         positions,
         neighbours,
         counts.reshape(1, -1),
-        send_lists[0],
+        send_lists.transpose(1, 0, 2),
         sparse_points,
         weights.reshape(-1, 128),
-        jnp.asarray(fold, BF16),
-        jnp.asarray(fold.T, BF16),
     )
     return energies.reshape(-1), forces
 

time: 73.8 us -> 65.1 us (0.88)
  the two profiles are of different devices: /device:TPU:18 before, /device:TPU:1 now
where the time goes in v1:
time: 65.1 us; the launch traced here: 65 us
  Pallas kernels  61.9 us (95%)
  local copies, waits for them, and re-layouts  2.39 us (4%)
    pallas_call x1, Pallas kernels, body(): pl.pallas_call(lambda *refs: kernel(faces, *refs), out_shape=(jax.ShapeDt...  61.9 us
    unnamed x2, local copies, waits for them, and re-layouts  2.39 us

profile of v1, /device:TPU:1, one launch (start us, length us, event | category | flops | bytes accessed | tf_op | source)
XLA Modules:
  0.0 65.0 jit_solution(14673002889269989434)
XLA Ops:
  0.6 61.9 %gap_forces.1 = (f32[1,64]{1,0:T(1,128)}, f32[3,64]{1,0:T(4,128)}) custom-call(f32[3,64]{1,0:T(4,128)} %refs_0_.1, s32[24,64]{1,0:T(8,128)} %refs_1_.1, s32[1,64]{1,0:T(1,128)} %bitcast.6, s32[6,1,128]{2,1,0:T(1,128)} %bitcast.5, bf16[2048,512]{1,0:T(8,128)(2,1)} %refs_4_.1, f32[16,128]{1,0:T(8,128)} %bitcast.4), custom_call_target="tpu_custom_call" | custom-call | tf_op jit(solution)/shard_map/gap_forces/pallas_call | solution.py:502
  62.6 1.1 %copy.10 = f32[64]{0:T(128)} copy(f32[64]{0:T(128)} %bitcast.7) | data formatting | bytes 512
  63.7 1.2 %copy.11 = f32[3,64]{1,0:T(4,128)} copy(f32[3,64]{1,0:T(4,128)} %get-tuple-element.9) | data formatting | bytes 1536

commit v2 on v1

--- a/solution.py
+++ b/solution.py
@@ -32,10 +32,7 @@
 ]
 
 
-def raised(m, axis):
-    p = list(POWERS[m])
-    p[axis] += 1
-    return PLACE[tuple(p)]
+FLAT = {(a, b): i for i, (a, b) in enumerate((a, b) for a in range(8) for b in range(8 - a))}
 
 
 def packed_place(e):
@@ -71,9 +68,9 @@
 
 def kernel(
     faces, pos_hbm, near_hbm, count_hbm, lists_hbm, sparse_hbm, weight_hbm,
-    energy_ref, force_ref,
+    out_ref,
     pos_ref, near_ref, count_ref, lists_ref, weight_ref,
-    posbuf, topbuf, ghost_out, tab, pack, index, ohs, oht, ohn, looked, offs, base, mono, radial, slope_r, dens,
+    posbuf, topbuf, ghost_out, tab, pack, index, ohs, oht, ohn, looked, offs, zpow, planar, radial, slope_r, dens,
     spec, dbuf, rbuf, gbuf, vbuf, descs, slopes, sparse, fold, spread, folded, wide, left, pulls,
     gtab, gret, domg, fin, topg, fintop,
     local_sem, pos_s, pos_r, top_s, top_r, gho_s, gho_r, des_s, des_r, gra_s, gra_r, ret_s, ret_r, fin_s, fin_r, fit_s, fit_r,
@@ -240,48 +237,48 @@
         c.wait()
     look(4, 4 + faces, True)
 
-    offs[...] = jnp.zeros(offs.shape, F32)
-    for j in range(SLOTS):
-        offs[j] = 0.5 * (looked[j] - here)
-    x, y, zz = offs[:, 0, :], offs[:, 1, :], offs[:, 2, :]
-    squared = x * x + y * y + zz * zz
-    j16 = lax.broadcasted_iota(jnp.int32, (16, 128), 0)
-    h16 = lax.broadcasted_iota(jnp.int32, (16, 128), 1) // 64
-    slot = jnp.where(j16 < 8, j16 + 8 * h16, 8 + j16 + 4 * h16)
     pack[0:8] = jnp.zeros((8, 128), jnp.int32)
     pack[0:1, 0:64] = count_ref[...]
     counts = pack[0:8]
-    counts = (counts + swap(counts))[0:1]
-    live = jnp.where((slot < counts) & (j16 < SLOTS), 1.0, 0.0)
-    inside = 1.0 - squared * (1.0 / 3.5)
-    base[0] = squared
-    base[1] = inside * inside * live
-    base[2] = (-2.0 / 3.5) * inside * live
-    mono[0] = jnp.ones((16, 128), F32)
-    for m in range(1, len(POWERS)):
-        p = list(POWERS[m])
-        axis = 2 if p[2] else 1 if p[1] else 0
-        by = (x, y, zz)[axis] * (1.0 / p[axis])
-        p[axis] -= 1
-        mono[m] = mono[PLACE[tuple(p)]] * by
+    counts = jnp.broadcast_to((counts + swap(counts))[0:1], (8, 128))
+    upper = lane // 64
     centre = 0.05 + 0.15 * row8.astype(F32)
     for j in range(SLOTS):
-        gap = base[0, j : j + 1, :] - centre
-        bell = jnp.exp(-30.0 * gap * gap)
-        r = bell * base[1, j : j + 1, :]
+        off = 0.5 * (looked[j] - here)
+        offs[j] = off
+        x, y, zz = (jnp.broadcast_to(off[axis : axis + 1], (8, 128)) for axis in range(3))
+        squared = x * x + y * y + zz * zz
+        slot = j + 8 * upper if j < 8 else 8 + j + 4 * upper
+        live = jnp.where(slot < counts, 1.0, 0.0)
+        inside = 1.0 - squared * (1.0 / 3.5)
+        gap = squared - centre
+        bell = jnp.exp(-30.0 * gap * gap) * live
+        r = bell * (inside * inside)
         radial[j] = r
-        slope_r[j] = r * (-60.0 * gap) + bell * base[2, j : j + 1, :]
-
-    @pl.loop(0, len(POWERS) // 8)
-    def _(block):
+        slope_r[j] = r * (-60.0 * gap) + bell * ((-2.0 / 3.5) * inside)
+        power = {0: None}
+        for c in range(1, 8):
+            power[c] = zz if c == 1 else power[c - 1] * (zz * (1.0 / c))
+            zpow[j, c - 1] = power[c]
+        ys = [None]
+        for c in range(1, 8):
+            ys.append(y if c == 1 else ys[c - 1] * (y * (1.0 / c)))
+        xs = None
+        for c in range(8):
+            xs = None if c == 0 else x if c == 1 else xs * (x * (1.0 / c))
+            for d in range(8 - c):
+                if c + d:
+                    planar[j, FLAT[c, d] - 1] = xs if d == 0 else ys[d] if c == 0 else xs * ys[d]
+
+    for (a, b), at in FLAT.items():
         rs = [radial[j] for j in range(SLOTS)]
-        for u in range(8):
-            m = block * 8 + u
-            rows = mono[m]
-            total = rs[0] * rows[0:1, :]
-            for j in range(1, SLOTS):
-                total = total + rs[j] * rows[j : j + 1, :]
-            dens[m] = total + swap(total)
+        if at:
+            rs = [r * planar[j, at - 1] for j, r in enumerate(rs)]
+        for c in range(8 - a - b):
+            terms = [r if c == 0 else r * zpow[j, c - 1] for j, r in enumerate(rs)]
+            while len(terms) > 1:
+                terms = [sum(terms[i : i + 2][1:], terms[i]) for i in range(0, len(terms), 2)]
+            dens[PLACE[a, b, c]] = terms[0] + swap(terms[0])
 
     def turned(d):
         return jnp.where(low, d, up(d, 2))
@@ -328,7 +325,7 @@
 
     wlow = lax.broadcasted_iota(jnp.int32, (ROWS, 128), 1) < 64
     sent_grad = [None] * 8
-    for slots in ((0, 1, 2, 3), (4, 5, 6, 7)):
+    for slots in ((7, 5, 6, 0), (3, 4, 1, 2)):
         for t in slots:
             if t:
                 sent_desc[t - 1].wait_recv()
@@ -373,7 +370,7 @@
         sent_grad[t].wait_recv()
         summed = summed + gbuf[t - 1].astype(F32)
     last = summed[ROWS : ROWS + 8, :]
-    energy_ref[...] = (0.25 * jnp.sum(last, axis=0, keepdims=True))[:, 0:64]
+    energy = 0.25 * jnp.sum(last, axis=0, keepdims=True)
 
     dot = jnp.zeros((8, 128), F32)
     for g in range(20):
@@ -395,23 +392,36 @@
             v = k1 * up(t, 1) + k2 * up(t, 2) + (k5 * up(t, 5) + k6 * up(t, 6))
             left[m] = (v + swap(v)) * SPREAD[m]
 
-    @pl.loop(0, SLOTS // 4)
+    @pl.loop(0, SLOTS // 3)
     def _(block):
-        q = [[None] * 4 for _ in range(4)]
+        js = [block * 3 + u for u in range(3)]
+        zp = [[None] + [zpow[j, c] for c in range(7)] for j in js]
+        q = [[None] * 3 for _ in range(4)]
 
         def add(old, new):
             return new if old is None else old + new
 
-        for m in range(len(POWERS)):
-            d = [left[m]]
-            if m < STARTS[7]:
-                d += [left[raised(m, axis)] for axis in range(3)]
-            for u in range(4):
-                b = mono[m, pl.ds(block * 4 + u, 1), :]
-                for axis in range(len(d)):
-                    q[axis][u] = add(q[axis][u], d[axis] * b)
-        for u in range(4):
-            j = block * 4 + u
+        def mul(tile, factor):
+            return tile if factor is None else tile * factor
+
+        for (a, b), at in FLAT.items():
+            level, deriv = [None] * 3, [None] * 3
+            for c in range(8 - a - b):
+                d = left[PLACE[a, b, c]]
+                for u in range(3):
+                    level[u] = add(level[u], mul(d, zp[u][c]))
+                    if c:
+                        deriv[u] = add(deriv[u], mul(d, zp[u][c - 1]))
+            for u, j in enumerate(js):
+                flat = planar[j, at - 1] if at else None
+                q[0][u] = add(q[0][u], mul(level[u], flat))
+                if deriv[u] is not None:
+                    q[3][u] = add(q[3][u], mul(deriv[u], flat))
+                for axis, lower in ((1, (a - 1, b)), (2, (a, b - 1))):
+                    if lower in FLAT:
+                        flat = planar[j, FLAT[lower] - 1] if FLAT[lower] else None
+                        q[axis][u] = add(q[axis][u], mul(level[u], flat))
+        for u, j in enumerate(js):
             r = radial[j]
             by_square = jnp.sum(slope_r[j] * q[0][u], axis=0, keepdims=True)
             gx, gy, gz = (jnp.sum(r * q[axis][u], axis=0, keepdims=True) for axis in (1, 2, 3))
@@ -488,7 +498,7 @@
         mine = mine + fin[d - 1]
     odd = jnp.where(lax.rem(sp, 2) == 1, 1, 0)
     mine = jnp.where(odd == 1, swap(mine), mine)
-    force_ref[...] = (centre_grad - mine)[0:3, 0:64]
+    out_ref[...] = jnp.where(row8 == 3, energy, centre_grad - mine)
     for c in sent_desc + sent_grad[1:] + sent_back + sent_top + sent_fin:
         c.wait_send()
 
@@ -499,14 +509,11 @@
     vmem = pl.BlockSpec(memory_space=pltpu.VMEM)
     hbm = pl.BlockSpec(memory_space=pl.ANY)
     dma = pltpu.SemaphoreType.DMA
-    energies, forces = pl.pallas_call(
+    out = pl.pallas_call(
         lambda *refs: kernel(faces, *refs),
-        out_shape=(
-            jax.ShapeDtypeStruct((1, 64), F32),
-            jax.ShapeDtypeStruct((3, 64), F32),
-        ),
+        out_shape=jax.ShapeDtypeStruct((8, 128), F32),
         in_specs=[hbm] * 6,
-        out_specs=(vmem, vmem),
+        out_specs=vmem,
         scratch_shapes=[
             pltpu.VMEM(positions.shape, F32),
             pltpu.VMEM(neighbours.shape, jnp.int32),
@@ -523,9 +530,9 @@
             pltpu.VMEM((128, 128), BF16),
             pltpu.VMEM((128, SLOTS * 128), BF16),
             pltpu.VMEM((SLOTS, 8, 128), F32),
-            pltpu.VMEM((16, 8, 128), F32),
-            pltpu.VMEM((3, 16, 128), F32),
-            pltpu.VMEM((120, 16, 128), F32),
+            pltpu.VMEM((SLOTS, 8, 128), F32),
+            pltpu.VMEM((SLOTS, 7, 8, 128), F32),
+            pltpu.VMEM((SLOTS, 35, 8, 128), F32),
             pltpu.VMEM((SLOTS, 8, 128), F32),
             pltpu.VMEM((SLOTS, 8, 128), F32),
             pltpu.VMEM((120, 8, 128), F32),
@@ -571,7 +578,7 @@
         sparse_points,
         weights.reshape(-1, 128),
     )
-    return energies.reshape(-1), forces
+    return out[3, 0:64], out[0:3, 0:64]
 
 
 def solution(mesh):

time: 65.1 us -> 64.6 us (level)
  the two profiles are of different devices: /device:TPU:1 before, /device:TPU:8 now
where the time goes in v2:
time: 64.6 us; the launch traced here: 64.3 us
  Pallas kernels  61.2 us (95%)
  local copies, waits for them, and re-layouts  2.45 us (4%)
    pallas_call x1, Pallas kernels, body(): pl.pallas_call(lambda *refs: kernel(faces, *refs), out_shape=jax.ShapeDty...  61.2 us

profile of v2, /device:TPU:8, one launch (start us, length us, event | category | flops | bytes accessed | tf_op | source)
XLA Modules:
  0.0 64.3 jit_solution(16933399512496782290)
XLA Ops:
  0.6 61.2 %gap_forces.1 = f32[8,128]{1,0:T(8,128)} custom-call(f32[3,64]{1,0:T(4,128)} %refs_0_.1, s32[24,64]{1,0:T(8,128)} %refs_1_.1, s32[1,64]{1,0:T(1,128)} %bitcast.7, s32[6,1,128]{2,1,0:T(1,128)} %bitcast.6, bf16[2048,512]{1,0:T(8,128)(2,1)} %refs_4_.1, f32[16,128]{1,0:T(8,128)} %bitcast.5), custom_call_target="tpu_custom_call" | custom-call | tf_op jit(solution)/shard_map/gap_forces/pallas_call | solution.py:512
  61.9 1.2 %slice_bitcast_fusion = f32[64]{0:T(128)} fusion(f32[8,128]{1,0:T(8,128)} %gap_forces.1), kind=kLoop, calls=%fused_computation | loop fusion | bytes 512 | tf_op jit(solution)/shard_map/squeeze | solution.py:581
  63.1 1.3 %slice.7 = f32[3,64]{1,0:T(4,128)} slice(f32[8,128]{1,0:T(8,128)} %gap_forces.1), slice={[0:3], [0:64]} | slice | bytes 1536 | tf_op jit(solution)/shard_map/slice | solution.py:581

commit v3 on v2

--- a/solution.py
+++ b/solution.py
@@ -10,9 +10,10 @@
 F32, BF16 = jnp.float32, jnp.bfloat16
 MESH = pl.DeviceIdType.MESH
 SLOTS = 12
-ROWS = 160
-BACK = 176
+ROWS = 144
+BACK = 160
 CHUNK = 512
+FAR = (7, 1, 6, 2, 5, 3, 4)
 
 
 def powers():
@@ -40,9 +41,13 @@
     r = (n2 - n) & 7
     first = jnp.where(r > 4, n2, n)
     r = jnp.where(r > 4, 8 - r, r)
-    group = jnp.where(r == 0, 16 + (l & 3), jnp.where((r & 1) == 1, l, 8 + l))
-    half = jnp.where(r == 0, l // 4, jnp.where(r > 2, 1, 0))
-    return half * ROWS + group * 8 + first
+    row = jnp.where(r == 4, (first & 3) + 4 * (l & 1), first)
+    diagonal = jnp.where(l < 4, 12 + l, 16 + (l & 1))
+    group = jnp.where(
+        r == 0, diagonal, jnp.where(r == 4, 8 + l // 2, jnp.where(r == 2, 8 + l, l))
+    )
+    half = jnp.where(r == 0, jnp.where((l == 4) | (l == 5), 0, 1), jnp.where(r > 2, 1, 0))
+    return half * ROWS + group * 8 + row
 
 
 def up(x, k):
@@ -70,7 +75,7 @@
     faces, pos_hbm, near_hbm, count_hbm, lists_hbm, sparse_hbm, weight_hbm,
     out_ref,
     pos_ref, near_ref, count_ref, lists_ref, weight_ref,
-    posbuf, topbuf, ghost_out, tab, pack, index, ohs, oht, ohn, looked, offs, zpow, planar, radial, slope_r, dens,
+    posbuf, topbuf, ghost_out, tab, pack, index, ohs, oht, ohn, looked, offs, zpow, planar, ahead, radial, slope_r, dens,
     spec, dbuf, rbuf, gbuf, vbuf, descs, slopes, sparse, fold, spread, folded, wide, left, pulls,
     gtab, gret, domg, fin, topg, fintop,
     local_sem, pos_s, pos_r, top_s, top_r, gho_s, gho_r, des_s, des_r, gra_s, gra_r, ret_s, ret_r, fin_s, fin_r, fit_s, fit_r,
@@ -102,6 +107,13 @@
     def above(d):
         return (lax.rem(dom + below, n_dom), lax.rem(sp + d, n_sp))
 
+    barrier = pltpu.get_barrier_semaphore()
+    greeted = [above(d) for d in (0, 1, 7, 2, 6, 3, 5, 4)] + [peer(d) for d in FAR]
+    greeted += [along(d) for d in (4, -4, 3, -3, 2, -2, 1, -1)]
+    greeted += [partner(f) for f in reversed(range(faces - 1))]
+    for who in greeted:
+        pl.semaphore_signal(barrier, inc=1, device_id=who, device_id_type=MESH)
+
     pairs = [
         (pos_hbm, pos_ref), (lists_hbm, lists_ref), (near_hbm, near_ref), (count_hbm, count_ref),
         (weight_hbm, weight_ref), (sparse_hbm, sparse),
@@ -109,12 +121,6 @@
     loads = [pltpu.make_async_copy(a, b, local_sem.at[i]) for i, (a, b) in enumerate(pairs)]
     for load in loads:
         load.start()
-
-    barrier = pltpu.get_barrier_semaphore()
-    greeted = [peer(d) for d in range(1, 8)] + [partner(f) for f in range(faces - 1)]
-    greeted += [along(d) for d in (1, -1, 2, -2, 3, -3, 4, -4)] + [above(d) for d in range(8)]
-    for who in greeted:
-        pl.semaphore_signal(barrier, inc=1, device_id=who, device_id_type=MESH)
 
     loads[0].wait()
     loads[1].wait()
@@ -148,14 +154,14 @@
         remote(posbuf.at[sp], posbuf.at[sp], pos_s.at[d - 1], pos_r.at[d - 1], peer(d))
         for d in range(1, 8)
     ]
-    for c in sent_pos:
-        c.start()
+    for d in FAR:
+        sent_pos[d - 1].start()
 
     sent_top = [
         remote(posbuf.at[sp], topbuf.at[sp], top_s.at[d], top_r.at[d], above(d)) for d in range(8)
     ]
-    for c in sent_top:
-        c.start()
+    for d in (0, 1, 7, 2, 6, 3, 5, 4):
+        sent_top[d].start()
 
     place = packed_place(lax.broadcasted_iota(jnp.int32, (8, 512), 1))[0:1]
     numbers = lax.broadcasted_iota(jnp.int32, (2 * ROWS, 512), 0)
@@ -283,24 +289,32 @@
     def turned(d):
         return jnp.where(low, d, up(d, 2))
 
-    zero = []
+    zero, four = [], []
     for l in range(8):
         s0 = s1 = s2 = None
         for m in range(STARTS[l], STARTS[l + 1]):
             d = dens[m]
             t = turned(d)
+            y1, y2 = up(t, 1), up(t, 2)
+            ahead[m, 0] = y1
+            ahead[m, 1] = y2
             f = d * SPREAD[m]
-            a, b, c = f * d, f * up(t, 1), f * up(t, 2)
+            a, b, c = f * d, f * y1, f * y2
             s0, s1, s2 = (a, b, c) if s0 is None else (s0 + a, s1 + b, s2 + c)
         spec[l] = s1
         spec[8 + l] = s2
         zero.append(s0)
+        four.append(s2)
     for l in range(4):
-        spec[16 + l] = jnp.where(low, zero[l], zero[l + 4])
+        pair = jnp.where(row8 < 4, four[2 * l], up(four[2 * l + 1], 4))
+        spec[8 + l] = jnp.where(low, spec[8 + l], pair)
+        spec[12 + l] = jnp.where(low, spec[12 + l], zero[l])
+    for l in range(2):
+        spec[16 + l] = jnp.where(low, zero[4 + l], zero[6 + l])
     twice = jnp.where(low, 2.0, 1.0)
 
     def times(g):
-        return 2.0 if g < 8 else twice if g < 16 else 1.0
+        return 2.0 if g < 12 else twice if g < 16 else 1.0
 
     def both(tile):
         row = jnp.sum(tile, axis=0, keepdims=True)
@@ -308,11 +322,11 @@
         return tile + swap(tile)
 
     total = jnp.zeros((8, 128), F32)
-    for g in range(20):
+    for g in range(18):
         v = spec[g]
         total = total + times(g) * v * v
     scale = lax.rsqrt(both(total) + 1e-06)
-    for g in range(0, 20, 2):
+    for g in range(0, 18, 2):
         two = jnp.concatenate([spec[g] * scale, spec[g + 1] * scale], axis=0)
         dbuf[0, g * 8 : g * 8 + 16, :] = two.astype(BF16)
 
@@ -373,23 +387,25 @@
     energy = 0.25 * jnp.sum(last, axis=0, keepdims=True)
 
     dot = jnp.zeros((8, 128), F32)
-    for g in range(20):
+    for g in range(18):
         dot = dot + summed[g * 8 : g * 8 + 8, :] * spec[g]
     dot = both(dot) * scale
     pull = []
-    for g in range(20):
+    for g in range(18):
         pull.append(scale * (summed[g * 8 : g * 8 + 8, :] - times(g) * (spec[g] * scale) * dot))
     for l in range(8):
-        ha, hb, h0 = pull[l], pull[8 + l], pull[16 + l % 4]
-        h0 = swap(h0) if l < 4 else h0
+        ha, hb = pull[l], pull[8 + l]
+        h0 = pull[12 + l] if l < 4 else swap(pull[12 + l]) if l < 6 else pull[10 + l]
+        pair = pull[8 + l // 2]
+        h4 = jnp.where((row8 < 4) == (l % 2 == 0), pair, up(pair, 4))
         other = swap(ha)
         k1 = ha
-        k2 = jnp.where(low, hb, hb + up(hb, 4))
-        k5 = jnp.where(low, up(other, -3), up(other, -1))
-        k6 = jnp.where(low, up(hb, -2), 2.0 * h0)
+        k2 = jnp.where(low, hb, h4)
+        k5 = up(jnp.where(low, up(other, -3), up(other, -1)), 4)
+        k6 = up(jnp.where(low, up(hb, -2), 2.0 * h0), 4)
         for m in range(STARTS[l], STARTS[l + 1]):
-            t = turned(dens[m])
-            v = k1 * up(t, 1) + k2 * up(t, 2) + (k5 * up(t, 5) + k6 * up(t, 6))
+            y1, y2 = ahead[m, 0], ahead[m, 1]
+            v = k1 * y1 + k2 * y2 + up(k5 * y1 + k6 * y2, 4)
             left[m] = (v + swap(v)) * SPREAD[m]
 
     @pl.loop(0, SLOTS // 3)
@@ -483,17 +499,17 @@
         c.wait_recv()
     which = [lists_ref[f] // 128 for f in range(top)]
     domg[...] = own + home([gret[f] for f in range(top)], which, ohs[...])
-    sent_fin = []
-    for d in range(1, 8):
+    sent_fin = [None] * 7
+    for d in FAR:
         who = peer(d)
         c = remote(domg.at[who[1] // 2], fin.at[d - 1], fin_s.at[d - 1], fin_r.at[d - 1], who)
         c.start()
-        sent_fin.append(c)
+        sent_fin[d - 1] = c
     mine = domg[sp // 2]
     for d in range(8):
         sent_top[d].wait_recv()
         mine = mine + fintop[d]
-    for d in range(1, 8):
+    for d in reversed(FAR):
         sent_fin[d - 1].wait_recv()
         mine = mine + fin[d - 1]
     odd = jnp.where(lax.rem(sp, 2) == 1, 1, 0)
@@ -501,6 +517,11 @@
     out_ref[...] = jnp.where(row8 == 3, energy, centre_grad - mine)
     for c in sent_desc + sent_grad[1:] + sent_back + sent_top + sent_fin:
         c.wait_send()
+
+
+def split_outputs(out_ref, energy_ref, force_ref):
+    energy_ref[...] = out_ref[3:4, 0:64]
+    force_ref[...] = out_ref[0:3, 0:64]
 
 
 def body(positions, neighbours, counts, send_lists, sparse_points, weights):
@@ -533,10 +554,11 @@
             pltpu.VMEM((SLOTS, 8, 128), F32),
             pltpu.VMEM((SLOTS, 7, 8, 128), F32),
             pltpu.VMEM((SLOTS, 35, 8, 128), F32),
+            pltpu.VMEM((120, 2, 8, 128), F32),
             pltpu.VMEM((SLOTS, 8, 128), F32),
             pltpu.VMEM((SLOTS, 8, 128), F32),
             pltpu.VMEM((120, 8, 128), F32),
-            pltpu.VMEM((20, 8, 128), F32),
+            pltpu.VMEM((18, 8, 128), F32),
             pltpu.VMEM((8, ROWS, 128), BF16),
             pltpu.VMEM((8, BACK, 128), BF16),
             pltpu.VMEM((7, BACK, 128), BF16),
@@ -578,7 +600,15 @@
         sparse_points,
         weights.reshape(-1, 128),
     )
-    return out[3, 0:64], out[0:3, 0:64]
+    energies, forces = pl.pallas_call(
+        split_outputs,
+        out_shape=(jax.ShapeDtypeStruct((1, 64), F32), jax.ShapeDtypeStruct((3, 64), F32)),
+        in_specs=[vmem],
+        out_specs=(vmem, vmem),
+        compiler_params=pltpu.CompilerParams(vmem_limit_bytes=60 * 2**20),
+        name="split_outputs",
+    )(out)
+    return energies.reshape(-1), forces
 
 
 def solution(mesh):

time: 64.6 us -> 58.4 us (0.904)
  the two profiles are of different devices: /device:TPU:8 before, /device:TPU:2 now
where the time goes in v3:
time: 58.4 us; the launch traced here: 58.2 us
  Pallas kernels  57.6 us (99%)
  between operations  0.64 us (1%)
    pallas_call x1, Pallas kernels, body(): pl.pallas_call(lambda *refs: kernel(faces, *refs), out_shape=jax.ShapeDty...  56.3 us
    pallas_call x1, Pallas kernels, body(): pl.pallas_call(split_outputs, out_shape=(jax.ShapeDtypeStruct((1, 64), F3...  1.26 us

profile of v3, /device:TPU:2, one launch (start us, length us, event | category | flops | bytes accessed | tf_op | source)
XLA Modules:
  0.0 58.2 jit_solution(7758962564349678622)
XLA Ops:
  0.6 56.3 %gap_forces.1.out_ref = f32[8,128]{1,0:T(8,128)} custom-call(f32[3,64]{1,0:T(4,128)} %refs_0_.1, s32[24,64]{1,0:T(8,128)} %refs_1_.1, s32[1,64]{1,0:T(1,128)} %bitcast.6, s32[6,1,128]{2,1,0:T(1,128)} %bitcast.5, bf16[2048,512]{1,0:T(8,128)(2,1)} %refs_4_.1, f32[16,128]{1,0:T(8,128)} %bitcast.4), custom_call_target="tpu_custom_call" | custom-call | tf_op jit(solution)/shard_map/gap_forces/pallas_call | solution.py:533
  57.0 1.3 %split_outputs.1 = (f32[1,64]{1,0:T(1,128)}, f32[3,64]{1,0:T(4,128)}) custom-call(f32[8,128]{1,0:T(8,128)} %gap_forces.1.out_ref), custom_call_target="tpu_custom_call" | custom-call | tf_op jit(solution)/shard_map/split_outputs/pallas_call | solution.py:603

commit v4 on v3

--- a/solution.py
+++ b/solution.py
@@ -109,7 +109,6 @@
 
     barrier = pltpu.get_barrier_semaphore()
     greeted = [above(d) for d in (0, 1, 7, 2, 6, 3, 5, 4)] + [peer(d) for d in FAR]
-    greeted += [along(d) for d in (4, -4, 3, -3, 2, -2, 1, -1)]
     greeted += [partner(f) for f in reversed(range(faces - 1))]
     for who in greeted:
         pl.semaphore_signal(barrier, inc=1, device_id=who, device_id_type=MESH)
@@ -125,6 +124,8 @@
     loads[0].wait()
     loads[1].wait()
     top = faces - 1
+    for buf in (posbuf, topbuf, tab, gret, fin, fintop):
+        buf[:, 4:8, :] = jnp.zeros((buf.shape[0], 4, 128), F32)
     posbuf[sp] = jnp.zeros((8, 128), F32)
     posbuf[sp, 0:3, 0:64] = pos_ref[...]
     here = posbuf[sp]
@@ -151,14 +152,14 @@
         )
 
     sent_pos = [
-        remote(posbuf.at[sp], posbuf.at[sp], pos_s.at[d - 1], pos_r.at[d - 1], peer(d))
+        remote(posbuf.at[sp, 0:4], posbuf.at[sp, 0:4], pos_s.at[d - 1], pos_r.at[d - 1], peer(d))
         for d in range(1, 8)
     ]
     for d in FAR:
         sent_pos[d - 1].start()
 
     sent_top = [
-        remote(posbuf.at[sp], topbuf.at[sp], top_s.at[d], top_r.at[d], above(d)) for d in range(8)
+        remote(posbuf.at[sp, 0:4], topbuf.at[sp, 0:4], top_s.at[d], top_r.at[d], above(d)) for d in range(8)
     ]
     for d in (0, 1, 7, 2, 6, 3, 5, 4):
         sent_top[d].start()
@@ -208,7 +209,7 @@
     sent_ghost = []
     for f in range(top):
         ghost_out[f] = chosen(out[:, f * 128 : (f + 1) * 128], lists_ref[f] // 128)
-        c = remote(ghost_out.at[f], tab.at[4 + f], gho_s.at[f], gho_r.at[f], partner(f))
+        c = remote(ghost_out.at[f, 0:4], tab.at[4 + f, 0:4], gho_s.at[f], gho_r.at[f], partner(f))
         c.start()
         sent_ghost.append(c)
 
@@ -339,7 +340,7 @@
 
     wlow = lax.broadcasted_iota(jnp.int32, (ROWS, 128), 1) < 64
     sent_grad = [None] * 8
-    for slots in ((7, 5, 6, 0), (3, 4, 1, 2)):
+    for slots in ((7, 5, 6, 3), (4, 1, 2, 0)):
         for t in slots:
             if t:
                 sent_desc[t - 1].wait_recv()
@@ -477,7 +478,7 @@
     gtab[4 : 4 + faces] = scatter(4, 4 + faces)
     sent_back = []
     for f in range(top):
-        c = remote(gtab.at[4 + f], gret.at[f], ret_s.at[f], ret_r.at[f], partner(f))
+        c = remote(gtab.at[4 + f, 0:4], gret.at[f, 0:4], ret_s.at[f], ret_r.at[f], partner(f))
         c.start()
         sent_back.append(c)
 
@@ -491,7 +492,7 @@
     sent_top = []
     for d in range(8):
         who = above(d)
-        c = remote(topg.at[who[1] // 2], fintop.at[d], fit_s.at[d], fit_r.at[d], who)
+        c = remote(topg.at[who[1] // 2, 0:4], fintop.at[d, 0:4], fit_s.at[d], fit_r.at[d], who)
         c.start()
         sent_top.append(c)
     own = scatter(0, 4)
@@ -502,7 +503,7 @@
     sent_fin = [None] * 7
     for d in FAR:
         who = peer(d)
-        c = remote(domg.at[who[1] // 2], fin.at[d - 1], fin_s.at[d - 1], fin_r.at[d - 1], who)
+        c = remote(domg.at[who[1] // 2, 0:4], fin.at[d - 1, 0:4], fin_s.at[d - 1], fin_r.at[d - 1], who)
         c.start()
         sent_fin[d - 1] = c
     mine = domg[sp // 2]

time: 58.4 us -> 58.3 us (level)
  the two profiles are of different devices: /device:TPU:2 before, /device:TPU:8 now
where the time goes in v4:
time: 58.3 us; the launch traced here: 58 us
  Pallas kernels  57.3 us (98%)
  between operations  0.64 us (1%)
    pallas_call x1, Pallas kernels, body(): pl.pallas_call(lambda *refs: kernel(faces, *refs), out_shape=jax.ShapeDty...  56.1 us
    pallas_call x1, Pallas kernels, body(): pl.pallas_call(split_outputs, out_shape=(jax.ShapeDtypeStruct((1, 64), F3...  1.26 us

profile of v4, /device:TPU:8, one launch (start us, length us, event | category | flops | bytes accessed | tf_op | source)
XLA Modules:
  0.0 58.0 jit_solution(18141001916025893747)
XLA Ops:
  0.6 56.1 %gap_forces.1.out_ref = f32[8,128]{1,0:T(8,128)} custom-call(f32[3,64]{1,0:T(4,128)} %refs_0_.1, s32[24,64]{1,0:T(8,128)} %refs_1_.1, s32[1,64]{1,0:T(1,128)} %bitcast.6, s32[6,1,128]{2,1,0:T(1,128)} %bitcast.5, bf16[2048,512]{1,0:T(8,128)(2,1)} %refs_4_.1, f32[16,128]{1,0:T(8,128)} %bitcast.4), custom_call_target="tpu_custom_call" | custom-call | tf_op jit(solution)/shard_map/gap_forces/pallas_call | solution.py:534
  56.7 1.3 %split_outputs.1 = (f32[1,64]{1,0:T(1,128)}, f32[3,64]{1,0:T(4,128)}) custom-call(f32[8,128]{1,0:T(8,128)} %gap_forces.1.out_ref), custom_call_target="tpu_custom_call" | custom-call | tf_op jit(solution)/shard_map/split_outputs/pallas_call | solution.py:604

commit v5 on v4

--- a/solution.py
+++ b/solution.py
@@ -13,6 +13,7 @@
 ROWS = 144
 BACK = 160
 CHUNK = 512
+DIRECT = (7, 1, 6, 2, 5, 3)
 FAR = (7, 1, 6, 2, 5, 3, 4)
 
 
@@ -75,10 +76,10 @@
     faces, pos_hbm, near_hbm, count_hbm, lists_hbm, sparse_hbm, weight_hbm,
     out_ref,
     pos_ref, near_ref, count_ref, lists_ref, weight_ref,
-    posbuf, topbuf, ghost_out, tab, pack, index, ohs, oht, ohn, looked, offs, zpow, planar, ahead, radial, slope_r, dens,
+    posbuf, topbuf, ghost_out, tab, pack, index, ohs, oht, ohp, ohn, looked, offs, zpow, planar, ahead, radial, slope_r, dens,
     spec, dbuf, rbuf, gbuf, vbuf, descs, slopes, sparse, fold, spread, folded, wide, left, pulls,
-    gtab, gret, domg, fin, topg, fintop,
-    local_sem, pos_s, pos_r, top_s, top_r, gho_s, gho_r, des_s, des_r, gra_s, gra_r, ret_s, ret_r, fin_s, fin_r, fit_s, fit_r,
+    gtab, gret, domg, fin, topg, fintop, domown, faceg, farin, total_ref,
+    local_sem, pos_s, pos_r, top_s, top_r, gho_s, gho_r, des_s, des_r, gra_s, gra_r, ret_s, ret_r, fin_s, fin_r, fit_s, fit_r, far_s, far_r,
 ):
     dom, sp = lax.axis_index("dom"), lax.axis_index("sp")
     n_dom, n_sp = lax.axis_size("dom"), lax.axis_size("sp")
@@ -104,6 +105,12 @@
     low = lane < 64
     row8 = lax.broadcasted_iota(jnp.int32, (8, 128), 0)
 
+    def sends_far(d):
+        return sp + d < n_sp if d >= 5 else sp + d >= n_sp
+
+    def gets_far(d):
+        return sp >= d if d >= 5 else sp < d
+
     def above(d):
         return (lax.rem(dom + below, n_dom), lax.rem(sp + d, n_sp))
 
@@ -112,6 +119,16 @@
     greeted += [partner(f) for f in reversed(range(faces - 1))]
     for who in greeted:
         pl.semaphore_signal(barrier, inc=1, device_id=who, device_id_type=MESH)
+    count = len(greeted)
+    for d in DIRECT:
+        count = count + (faces - 1) * jnp.where(sends_far(d), 1, 0)
+
+        @pl.when(sends_far(d))
+        def _():
+            for f in range(faces - 1):
+                who = (partner(f)[0], lax.rem(sp + d, n_sp))
+                pl.semaphore_signal(barrier, inc=1, device_id=who, device_id_type=MESH)
+
 
     pairs = [
         (pos_hbm, pos_ref), (lists_hbm, lists_ref), (near_hbm, near_ref), (count_hbm, count_ref),
@@ -144,7 +161,7 @@
     index[8:16] = jnp.where(row8 < 4, last, 0)
     for j in range(SLOTS):
         ohn[:, j * 128 : (j + 1) * 128] = one_hot(index[j : j + 1, :] & 127)
-    pl.semaphore_wait(barrier, len(greeted))
+    pl.semaphore_wait(barrier, count)
 
     def remote(src, dst, s, r, who):
         return pltpu.make_async_remote_copy(
@@ -208,7 +225,8 @@
     out = gather(tab[0:4], ohs[...])
     sent_ghost = []
     for f in range(top):
-        ghost_out[f] = chosen(out[:, f * 128 : (f + 1) * 128], lists_ref[f] // 128)
+        tile = chosen(out[:, f * 128 : (f + 1) * 128], lists_ref[f] // 128)
+        ghost_out[f] = jnp.where(row8 == 3, lists_ref[f].astype(F32), tile)
         c = remote(ghost_out.at[f, 0:4], tab.at[4 + f, 0:4], gho_s.at[f], gho_r.at[f], partner(f))
         c.start()
         sent_ghost.append(c)
@@ -337,6 +355,10 @@
     ]
     for t in (7, 5, 6, 3, 4, 1, 2):
         sent_desc[t - 1].start()
+
+    partner_lists = [tab[4 + f, 3:4, :].astype(jnp.int32) for f in range(top)]
+    for f in range(top):
+        ohp[:, f * 128 : (f + 1) * 128] = one_hot(partner_lists[f] & 127)
 
     wlow = lax.broadcasted_iota(jnp.int32, (ROWS, 128), 1) < 64
     sent_grad = [None] * 8
@@ -496,27 +518,70 @@
         c.start()
         sent_top.append(c)
     own = scatter(0, 4)
+    domown[...] = own
+    def final(src, d):
+        who = peer(d)
+        return remote(
+            src.at[who[1] // 2, 0:4], fin.at[d - 1, 0:4], fin_s.at[d - 1], fin_r.at[d - 1], who
+        )
+
+    sent_fin = {d: final(domg, d) for d in FAR}
+    for d in DIRECT:
+        pl.when(sends_far(d))(final(domown, d).start)
+    for f in range(top):
+        hots = ohp[:, f * 128 : (f + 1) * 128]
+        faceg[f] = home([gtab[4 + f]], [partner_lists[f] // 128], hots)
+    sent_far = {}
+    for k, d in enumerate(DIRECT):
+        there = lax.rem(sp + d, n_sp)
+        sent_far[d] = [
+            remote(
+                faceg.at[f, there // 2, 0:4], farin.at[f, k, 0:4],
+                far_s.at[f * 6 + k], far_r.at[f * 6 + k], (partner(f)[0], there),
+            )
+            for f in range(top)
+        ]
+
+        @pl.when(sends_far(d))
+        def _():
+            for c in sent_far[d]:
+                c.start()
+
     for c in sent_back:
         c.wait_recv()
     which = [lists_ref[f] // 128 for f in range(top)]
     domg[...] = own + home([gret[f] for f in range(top)], which, ohs[...])
-    sent_fin = [None] * 7
     for d in FAR:
-        who = peer(d)
-        c = remote(domg.at[who[1] // 2, 0:4], fin.at[d - 1, 0:4], fin_s.at[d - 1], fin_r.at[d - 1], who)
-        c.start()
-        sent_fin[d - 1] = c
+        if d in DIRECT:
+            pl.when(jnp.logical_not(sends_far(d)))(sent_fin[d].start)
+        else:
+            sent_fin[d].start()
     mine = domg[sp // 2]
     for d in range(8):
         sent_top[d].wait_recv()
         mine = mine + fintop[d]
     for d in reversed(FAR):
-        sent_fin[d - 1].wait_recv()
+        sent_fin[d].wait_recv()
         mine = mine + fin[d - 1]
+    total_ref[...] = mine
+    for k, d in enumerate(DIRECT):
+
+        @pl.when(gets_far(d))
+        def _():
+            for f in range(top):
+                sent_far[d][f].wait_recv()
+                total_ref[0:4, :] = total_ref[0:4, :] + farin[f, k, 0:4, :]
+
+        @pl.when(sends_far(d))
+        def _():
+            for c in sent_far[d]:
+                c.wait_send()
+
+    mine = total_ref[...]
     odd = jnp.where(lax.rem(sp, 2) == 1, 1, 0)
     mine = jnp.where(odd == 1, swap(mine), mine)
     out_ref[...] = jnp.where(row8 == 3, energy, centre_grad - mine)
-    for c in sent_desc + sent_grad[1:] + sent_back + sent_top + sent_fin:
+    for c in sent_desc + sent_grad[1:] + sent_back + sent_top + list(sent_fin.values()):
         c.wait_send()
 
 
@@ -550,6 +615,7 @@
             pltpu.VMEM((16, 128), jnp.int32),
             pltpu.VMEM((128, (faces - 1) * 128), BF16),
             pltpu.VMEM((128, 128), BF16),
+            pltpu.VMEM((128, (faces - 1) * 128), BF16),
             pltpu.VMEM((128, SLOTS * 128), BF16),
             pltpu.VMEM((SLOTS, 8, 128), F32),
             pltpu.VMEM((SLOTS, 8, 128), F32),
@@ -579,6 +645,10 @@
             pltpu.VMEM((7, 8, 128), F32),
             pltpu.VMEM((4, 8, 128), F32),
             pltpu.VMEM((8, 8, 128), F32),
+            pltpu.VMEM((4, 8, 128), F32),
+            pltpu.VMEM((faces - 1, 4, 8, 128), F32),
+            pltpu.VMEM((faces - 1, 6, 8, 128), F32),
+            pltpu.VMEM((8, 128), F32),
             dma((6,)),
             dma((7,)), dma((7,)),
             dma((8,)), dma((8,)),
@@ -588,6 +658,7 @@
             dma((faces - 1,)), dma((faces - 1,)),
             dma((7,)), dma((7,)),
             dma((8,)), dma((8,)),
+            dma(((faces - 1) * 6,)), dma(((faces - 1) * 6,)),
         ],
         compiler_params=pltpu.CompilerParams(
             collective_id=0, has_side_effects=True, vmem_limit_bytes=60 * 2**20

time: 58.3 us -> 57.4 us (0.985)
  Pallas kernels: 57.3 us -> 56.6 us
    pallas_call x1, Pallas kernels: 56.1 us -> 55.4 us  [body(): pl.pallas_call(lambda *refs: kernel(faces, *refs), out_shape=jax.ShapeDty...]
where the time goes in v5:
time: 57.4 us; the launch traced here: 57.3 us
  Pallas kernels  56.6 us (99%)
  between operations  0.64 us (1%)
    pallas_call x1, Pallas kernels, body(): pl.pallas_call(lambda *refs: kernel(faces, *refs), out_shape=jax.ShapeDty...  55.4 us
    pallas_call x1, Pallas kernels, body(): pl.pallas_call(split_outputs, out_shape=(jax.ShapeDtypeStruct((1, 64), F3...  1.26 us

profile of v5, /device:TPU:8, one launch (start us, length us, event | category | flops | bytes accessed | tf_op | source)
XLA Modules:
  0.0 57.3 jit_solution(17662209489346416085)
XLA Ops:
  0.6 55.4 %gap_forces.1.out_ref = f32[8,128]{1,0:T(8,128)} custom-call(f32[3,64]{1,0:T(4,128)} %refs_0_.1, s32[24,64]{1,0:T(8,128)} %refs_1_.1, s32[1,64]{1,0:T(1,128)} %bitcast.6, s32[6,1,128]{2,1,0:T(1,128)} %bitcast.5, bf16[2048,512]{1,0:T(8,128)(2,1)} %refs_4_.1, f32[16,128]{1,0:T(8,128)} %bitcast.4), custom_call_target="tpu_custom_call" | custom-call | tf_op jit(solution)/shard_map/gap_forces/pallas_call | solution.py:599
  56.0 1.3 %split_outputs.1 = (f32[1,64]{1,0:T(1,128)}, f32[3,64]{1,0:T(4,128)}) custom-call(f32[8,128]{1,0:T(8,128)} %gap_forces.1.out_ref), custom_call_target="tpu_custom_call" | custom-call | tf_op jit(solution)/shard_map/split_outputs/pallas_call | solution.py:675

commit v6 on v5

--- a/solution.py
+++ b/solution.py
@@ -11,7 +11,6 @@
 MESH = pl.DeviceIdType.MESH
 SLOTS = 12
 ROWS = 144
-BACK = 160
 CHUNK = 512
 DIRECT = (7, 1, 6, 2, 5, 3)
 FAR = (7, 1, 6, 2, 5, 3, 4)
@@ -77,9 +76,9 @@
     out_ref,
     pos_ref, near_ref, count_ref, lists_ref, weight_ref,
     posbuf, topbuf, ghost_out, tab, pack, index, ohs, oht, ohp, ohn, looked, offs, zpow, planar, ahead, radial, slope_r, dens,
-    spec, dbuf, rbuf, gbuf, vbuf, descs, slopes, sparse, fold, spread, folded, wide, left, pulls,
+    spec, dbuf, rbuf, gbuf, eout, ein, vbuf, descs, slopes, sparse, fold, spread, folded, wide, left, pulls,
     gtab, gret, domg, fin, topg, fintop, domown, faceg, farin, total_ref,
-    local_sem, pos_s, pos_r, top_s, top_r, gho_s, gho_r, des_s, des_r, gra_s, gra_r, ret_s, ret_r, fin_s, fin_r, fit_s, fit_r, far_s, far_r,
+    local_sem, pos_s, pos_r, top_s, top_r, gho_s, gho_r, des_s, des_r, gra_s, gra_r, ret_s, ret_r, fin_s, fin_r, fit_s, fit_r, far_s, far_r, ene_s, ene_r,
 ):
     dom, sp = lax.axis_index("dom"), lax.axis_index("sp")
     n_dom, n_sp = lax.axis_size("dom"), lax.axis_size("sp")
@@ -361,7 +360,7 @@
         ohp[:, f * 128 : (f + 1) * 128] = one_hot(partner_lists[f] & 127)
 
     wlow = lax.broadcasted_iota(jnp.int32, (ROWS, 128), 1) < 64
-    sent_grad = [None] * 8
+    sent_grad, sent_energy = [None] * 8, [None] * 8
     for slots in ((7, 5, 6, 3), (4, 1, 2, 0)):
         for t in slots:
             if t:
@@ -388,27 +387,28 @@
             a, b = slots[2 * k], slots[2 * k + 1]
             at = slice(k * 128, (k + 1) * 128)
             lo, hi = grad[0:ROWS, at], grad[ROWS : 2 * ROWS, at]
-            rbuf[a, 0:ROWS, :] = jnp.where(wlow, lo, swap(hi)).astype(BF16)
-            rbuf[b, 0:ROWS, :] = jnp.where(wlow, swap(lo), hi).astype(BF16)
+            rbuf[a] = jnp.where(wlow, lo, swap(hi)).astype(BF16)
+            rbuf[b] = jnp.where(wlow, swap(lo), hi).astype(BF16)
             e = jnp.broadcast_to(energy[:, at], (8, 128))
             for t, mine in ((a, e), (b, swap(e))):
-                p = pieces(mine, 3)
-                tile = jnp.where(row8 == 0, p[0], jnp.where(row8 == 1, p[1], jnp.where(row8 == 2, p[2], 0.0)))
-                tile = jnp.concatenate([tile, jnp.zeros((8, 128), F32)], axis=0)
-                rbuf[t, ROWS:BACK, :] = tile.astype(BF16)
+                eout[t] = mine
         for t in slots:
             if t:
                 c = remote(rbuf.at[t], gbuf.at[t - 1], gra_s.at[t - 1], gra_r.at[t - 1], along(-delta[t]))
                 c.start()
                 sent_grad[t] = c
+        for t in slots:
+            if t:
+                c = remote(
+                    eout.at[t, 0:1], ein.at[t - 1, 0:1], ene_s.at[t - 1], ene_r.at[t - 1], along(-delta[t])
+                )
+                c.start()
+                sent_energy[t] = c
 
     summed = rbuf[0].astype(F32)
     for t in range(1, 8):
         sent_grad[t].wait_recv()
         summed = summed + gbuf[t - 1].astype(F32)
-    last = summed[ROWS : ROWS + 8, :]
-    energy = 0.25 * jnp.sum(last, axis=0, keepdims=True)
-
     dot = jnp.zeros((8, 128), F32)
     for g in range(18):
         dot = dot + summed[g * 8 : g * 8 + 8, :] * spec[g]
@@ -577,11 +577,16 @@
             for c in sent_far[d]:
                 c.wait_send()
 
+    energy = eout[0, 0:1, :]
+    for t in range(1, 8):
+        sent_energy[t].wait_recv()
+        energy = energy + ein[t - 1, 0:1, :]
+    energy = 0.25 * energy
     mine = total_ref[...]
     odd = jnp.where(lax.rem(sp, 2) == 1, 1, 0)
     mine = jnp.where(odd == 1, swap(mine), mine)
     out_ref[...] = jnp.where(row8 == 3, energy, centre_grad - mine)
-    for c in sent_desc + sent_grad[1:] + sent_back + sent_top + list(sent_fin.values()):
+    for c in sent_desc + sent_grad[1:] + sent_energy[1:] + sent_back + sent_top + list(sent_fin.values()):
         c.wait_send()
 
 
@@ -627,8 +632,10 @@
             pltpu.VMEM((120, 8, 128), F32),
             pltpu.VMEM((18, 8, 128), F32),
             pltpu.VMEM((8, ROWS, 128), BF16),
-            pltpu.VMEM((8, BACK, 128), BF16),
-            pltpu.VMEM((7, BACK, 128), BF16),
+            pltpu.VMEM((8, ROWS, 128), BF16),
+            pltpu.VMEM((7, ROWS, 128), BF16),
+            pltpu.VMEM((8, 8, 128), F32),
+            pltpu.VMEM((7, 8, 128), F32),
             pltpu.VMEM((2 * ROWS, 256), BF16),
             pltpu.VMEM((512, 256), BF16),
             pltpu.VMEM((points, 256), BF16),
@@ -659,6 +666,7 @@
             dma((7,)), dma((7,)),
             dma((8,)), dma((8,)),
             dma(((faces - 1) * 6,)), dma(((faces - 1) * 6,)),
+            dma((7,)), dma((7,)),
         ],
         compiler_params=pltpu.CompilerParams(
             collective_id=0, has_side_effects=True, vmem_limit_bytes=60 * 2**20

time: 57.4 us -> 57.2 us (level)
  no operation moved by 1% of the time
where the time goes in v6:
time: 57.2 us; the launch traced here: 57 us
  Pallas kernels  56.4 us (99%)
  between operations  0.64 us (1%)
    pallas_call x1, Pallas kernels, body(): pl.pallas_call(lambda *refs: kernel(faces, *refs), out_shape=jax.ShapeDty...  55.1 us
    pallas_call x1, Pallas kernels, body(): pl.pallas_call(split_outputs, out_shape=(jax.ShapeDtypeStruct((1, 64), F3...  1.26 us

profile of v6, /device:TPU:8, one launch (start us, length us, event | category | flops | bytes accessed | tf_op | source)
XLA Modules:
  0.0 57.0 jit_solution(1363821262713145704)
XLA Ops:
  0.6 55.1 %gap_forces.1.out_ref = f32[8,128]{1,0:T(8,128)} custom-call(f32[3,64]{1,0:T(4,128)} %refs_0_.1, s32[24,64]{1,0:T(8,128)} %refs_1_.1, s32[1,64]{1,0:T(1,128)} %bitcast.6, s32[6,1,128]{2,1,0:T(1,128)} %bitcast.5, bf16[2048,512]{1,0:T(8,128)(2,1)} %refs_4_.1, f32[16,128]{1,0:T(8,128)} %bitcast.4), custom_call_target="tpu_custom_call" | custom-call | tf_op jit(solution)/shard_map/gap_forces/pallas_call | solution.py:604
  55.8 1.3 %split_outputs.1 = (f32[1,64]{1,0:T(1,128)}, f32[3,64]{1,0:T(4,128)}) custom-call(f32[8,128]{1,0:T(8,128)} %gap_forces.1.out_ref), custom_call_target="tpu_custom_call" | custom-call | tf_op jit(solution)/shard_map/split_outputs/pallas_call | solution.py:683

commit v7 on v6

--- a/solution.py
+++ b/solution.py
@@ -381,8 +381,9 @@
             ws = jnp.concatenate([w, w], axis=1) * square
             energy = energy + jnp.sum((ws * square).reshape(CHUNK // 8, 8, 256), axis=0)
             slopes[at, :] = (ws * score).astype(BF16)
+            part = jnp.dot(folded[:, at], slopes[at, :], preferred_element_type=F32)
+            grad = part if c == 0 else grad + part
         energy = jnp.sum(energy, axis=0, keepdims=True)
-        grad = jnp.dot(folded[...], slopes[...], preferred_element_type=F32)
         for k in range(2):
             a, b = slots[2 * k], slots[2 * k + 1]
             at = slice(k * 128, (k + 1) * 128)
@@ -431,11 +432,11 @@
             v = k1 * y1 + k2 * y2 + up(k5 * y1 + k6 * y2, 4)
             left[m] = (v + swap(v)) * SPREAD[m]
 
-    @pl.loop(0, SLOTS // 3)
+    @pl.loop(0, SLOTS // 6)
     def _(block):
-        js = [block * 3 + u for u in range(3)]
+        js = [block * 6 + u for u in range(6)]
         zp = [[None] + [zpow[j, c] for c in range(7)] for j in js]
-        q = [[None] * 3 for _ in range(4)]
+        q = [[None] * 6 for _ in range(4)]
 
         def add(old, new):
             return new if old is None else old + new
@@ -444,10 +445,10 @@
             return tile if factor is None else tile * factor
 
         for (a, b), at in FLAT.items():
-            level, deriv = [None] * 3, [None] * 3
+            level, deriv = [None] * 6, [None] * 6
             for c in range(8 - a - b):
                 d = left[PLACE[a, b, c]]
-                for u in range(3):
+                for u in range(6):
                     level[u] = add(level[u], mul(d, zp[u][c]))
                     if c:
                         deriv[u] = add(deriv[u], mul(d, zp[u][c - 1]))

time: 57.2 us -> 57.1 us (level)
  no operation moved by 1% of the time
where the time goes in v7:
time: 57.1 us; the launch traced here: 56.9 us
  Pallas kernels  56.3 us (99%)
  between operations  0.64 us (1%)
    pallas_call x1, Pallas kernels, body(): pl.pallas_call(lambda *refs: kernel(faces, *refs), out_shape=jax.ShapeDty...  55 us
    pallas_call x1, Pallas kernels, body(): pl.pallas_call(split_outputs, out_shape=(jax.ShapeDtypeStruct((1, 64), F3...  1.26 us

profile of v7, /device:TPU:8, one launch (start us, length us, event | category | flops | bytes accessed | tf_op | source)
XLA Modules:
  0.0 56.9 jit_solution(5955658487038730849)
XLA Ops:
  0.6 55.0 %gap_forces.1.out_ref = f32[8,128]{1,0:T(8,128)} custom-call(f32[3,64]{1,0:T(4,128)} %refs_0_.1, s32[24,64]{1,0:T(8,128)} %refs_1_.1, s32[1,64]{1,0:T(1,128)} %bitcast.6, s32[6,1,128]{2,1,0:T(1,128)} %bitcast.5, bf16[2048,512]{1,0:T(8,128)(2,1)} %refs_4_.1, f32[16,128]{1,0:T(8,128)} %bitcast.4), custom_call_target="tpu_custom_call" | custom-call | tf_op jit(solution)/shard_map/gap_forces/pallas_call | solution.py:605
  55.7 1.3 %split_outputs.1 = (f32[1,64]{1,0:T(1,128)}, f32[3,64]{1,0:T(4,128)}) custom-call(f32[8,128]{1,0:T(8,128)} %gap_forces.1.out_ref), custom_call_target="tpu_custom_call" | custom-call | tf_op jit(solution)/shard_map/split_outputs/pallas_call | solution.py:684
